TPU v7x, 32 devices: a whole 2x2x4 slice. The times are simulated.
32 devices in a mesh: seq: 4 (over y, x), head: 8 (over z, core).
Axes of the slice: x: 2, y: 2, z: 4, core: 2. Of those that a mesh axis runs over, the one named last changes fastest.
Arguments:
- layer_input: bfloat16 [8192, 2048], P(('seq', 'head')), may hold values from -6 to 6
- mem_count: int32 [4], P('seq'), may hold values from 0 to 150, as said below
- text_len: int32 [4], P('seq'), may hold values from 924 to 1848
- slot_count: int32 [4], P('seq'), may hold values from 1 to 50
- w_query: bfloat16 [2048, 2048], P(None, 'head'), may hold values from -0.125 to 0.125
- w_key: bfloat16 [2048, 2048], P(None, 'head'), may hold values from -0.125 to 0.125
- w_value: bfloat16 [2048, 2048], P(None, 'head'), may hold values from -0.125 to 0.125
- b_query: bfloat16 [2048], P('head'), may hold values from -2 to 2
- b_value: bfloat16 [2048], P('head'), may hold values from -0.29882812 to 0.29882812
- ln1_gain: bfloat16 [2048], P(('seq', 'head')), may hold values from 0.5 to 1.5
- ln1_bias: bfloat16 [2048], P(('seq', 'head')), may hold values from -2 to 2
- w_out: bfloat16 [2048, 2048], P(('seq', 'head')), may hold values from -1 to 1
- b_out: bfloat16 [2048], P(('seq', 'head')), may hold values from -2 to 2
- ln2_gain: bfloat16 [2048], P(('seq', 'head')), may hold values from 0.5 to 1.5
- ln2_bias: bfloat16 [2048], P(('seq', 'head')), may hold values from -2 to 2
- w_up: bfloat16 [2048, 8192], P(None, ('seq', 'head')), may hold values from -0.125 to 0.125
- b_up: bfloat16 [8192], P(('seq', 'head')), may hold values from -3 to 3
- w_down: bfloat16 [8192, 2048], P(('seq', 'head')), may hold values from -0.0625 to 0.0625
- b_down: bfloat16 [2048], P(('seq', 'head')), may hold values from -2 to 2
- cotangent: bfloat16 [8192, 2048], P(('seq', 'head')), may hold values from -6 to 6
Outputs:
- out: bfloat16 [8192, 2048], P(('seq', 'head'))
- grad_input: bfloat16 [8192, 2048], P(('seq', 'head'))
- grad_w_query: float32 [2048, 2048], P(None, 'head')
- grad_w_key: float32 [2048, 2048], P(None, 'head')
- grad_w_value: float32 [2048, 2048], P(None, 'head')
- grad_b_query: float32 [2048], P('head')
- grad_b_value: float32 [2048], P('head')
- grad_ln1_gain: float32 [2048], P(('seq', 'head'))
- grad_ln1_bias: float32 [2048], P(('seq', 'head'))
- grad_w_out: float32 [2048, 2048], P(('seq', 'head'))
- grad_b_out: float32 [2048], P(('seq', 'head'))
- grad_ln2_gain: float32 [2048], P(('seq', 'head'))
- grad_ln2_bias: float32 [2048], P(('seq', 'head'))
- grad_w_up: float32 [2048, 8192], P(None, ('seq', 'head'))
- grad_b_up: float32 [8192], P(('seq', 'head'))
- grad_w_down: float32 [8192, 2048], P(('seq', 'head'))
- grad_b_down: float32 [2048], P(('seq', 'head'))
Inputs may be any that keep to these rules, and one draw needn't show every extreme that they name: `mem_count`: one sequence has 150 memories, 1848 text positions and 50 summary slots.
All inputs are finite; a program needn't handle non-finite values.
Results may differ from a plain program's by a relative error of at most 0.017.
Values may be sent and summed in bfloat16 or wider, within the bound.
No kernel may reach another device: no remote copies, remote signals or barrier semaphores. Data moves between devices by JAX's collectives and lax.ppermute only.
A program may use at most 384 MiB of HBM per device.

v0:
```python
import jax
import jax.numpy as jnp
from jax import lax
from jax.sharding import PartitionSpec as P

HEAD_DIM = 64
LENGTH = 2048


EPS = 1e-05
NEG = -1e30
FLOAT = jnp.float32
LOWER = jnp.bfloat16


def layer_norm(values, ln_gain, ln_shift):
    average = jnp.mean(values, axis=-1, keepdims=True)
    centred = values - average
    variance = jnp.mean(centred * centred, axis=-1, keepdims=True)
    return centred * lax.rsqrt(variance + EPS) * ln_gain + ln_shift


def exact_gelu(values):
    return jax.nn.gelu(values, approximate=False)


def visible(first, block_rows, length, memory, text_count, slot_num):
    query_pos = first + lax.broadcasted_iota(jnp.int32, (block_rows, length), 0)
    key_pos = lax.broadcasted_iota(jnp.int32, (block_rows, length), 1)
    key_valid = (key_pos < memory + text_count) | (key_pos >= length - slot_num)
    earlier = (key_pos <= query_pos) | (key_pos < memory)
    return key_valid & earlier | (key_pos == query_pos)


def contract_rows(left, right):
    return lax.dot_general(left, right, (((0,), (0,)), ((), ())), preferred_element_type=FLOAT)


def contract_cols(left, right):
    return lax.dot_general(left, right, (((1,), (1,)), ((), ())), preferred_element_type=FLOAT)


def block_inputs(index, query, keys, values, mem_count, text_len, slot_count, block_rows, per_seq):
    seq_idx = index // per_seq
    first = index % per_seq * block_rows
    start = seq_idx * LENGTH
    q_blk = lax.dynamic_slice_in_dim(query, start + first, block_rows, 0)
    k_seq = lax.dynamic_slice_in_dim(keys, start, LENGTH, 0)
    v_seq = lax.dynamic_slice_in_dim(values, start, LENGTH, 0)
    scores = jnp.einsum("qhd,khd->hqk", q_blk, k_seq, preferred_element_type=FLOAT)
    allowed = visible(
        first, block_rows, LENGTH, mem_count[seq_idx], text_len[seq_idx], slot_count[seq_idx]
    )
    scores = jnp.where(allowed[None], scores, NEG)
    return (start, first, q_blk, k_seq, v_seq, scores)


def attention_forward(query, keys, values, mem_count, text_len, slot_count):
    block_rows = min(512, LENGTH)
    per_seq = LENGTH // block_rows
    blocks_all = query.shape[0] // LENGTH * per_seq

    def one_block(index):
        start, first, q_blk, k_seq, v_seq, scores = block_inputs(
            index, query, keys, values, mem_count, text_len, slot_count, block_rows, per_seq
        )
        top = jnp.max(scores, axis=-1, keepdims=True)
        expo = jnp.exp(scores - top)
        total = jnp.sum(expo, axis=-1, keepdims=True)
        probs = (expo / total).astype(LOWER)
        context = jnp.einsum("hqk,khd->qhd", probs, v_seq, preferred_element_type=FLOAT)
        return (context.astype(LOWER), (top + jnp.log(total))[..., 0])

    context, logsum = lax.map(one_block, jnp.arange(blocks_all, dtype=jnp.int32))
    return (context.reshape(query.shape), logsum)


def attention_backward(query, keys, values, grad_context, logsum, mem_count, text_len, slot_count):
    block_rows = min(512, LENGTH)
    per_seq = LENGTH // block_rows
    blocks_all = query.shape[0] // LENGTH * per_seq

    def one_block(carry, inputs):
        grad_keys, grad_values = carry
        index, block_sum = inputs
        start, first, q_blk, k_seq, v_seq, scores = block_inputs(
            index, query, keys, values, mem_count, text_len, slot_count, block_rows, per_seq
        )
        probs = jnp.exp(scores - block_sum[..., None])
        probs_low = probs.astype(LOWER)
        grad_blk = lax.dynamic_slice_in_dim(grad_context, start + first, block_rows, 0)
        grad_probs = jnp.einsum("qhd,khd->hqk", grad_blk, v_seq, preferred_element_type=FLOAT)
        centre = jnp.sum(probs * grad_probs, axis=-1, keepdims=True)
        grad_scores = (probs * (grad_probs - centre)).astype(LOWER)
        grad_q = jnp.einsum("hqk,khd->qhd", grad_scores, k_seq, preferred_element_type=FLOAT)
        part_k = jnp.einsum("hqk,qhd->khd", grad_scores, q_blk, preferred_element_type=FLOAT)
        part_v = jnp.einsum("hqk,qhd->khd", probs_low, grad_blk, preferred_element_type=FLOAT)
        grad_keys = lax.dynamic_update_slice_in_dim(
            grad_keys, lax.dynamic_slice_in_dim(grad_keys, start, LENGTH, 0) + part_k, start, 0
        )
        grad_values = lax.dynamic_update_slice_in_dim(
            grad_values, lax.dynamic_slice_in_dim(grad_values, start, LENGTH, 0) + part_v, start, 0
        )
        return ((grad_keys, grad_values), grad_q)

    empty = jnp.zeros(keys.shape, FLOAT)
    (grad_keys, grad_values), grad_query = lax.scan(
        one_block, (empty, empty), (jnp.arange(blocks_all, dtype=jnp.int32), logsum)
    )
    return (grad_query.reshape(query.shape), grad_keys, grad_values)


def body(
    layer_input,
    mem_count,
    text_len,
    slot_count,
    w_query,
    w_key,
    w_value,
    b_query,
    b_value,
    ln1_gain,
    ln1_bias,
    w_out,
    b_out,
    ln2_gain,
    ln2_bias,
    w_up,
    b_up,
    w_down,
    b_down,
    cotangent,
):
    scale = HEAD_DIM ** (-0.5)
    local_width = w_query.shape[1]
    local_heads = local_width // HEAD_DIM
    gathered = (
        lax.all_gather(ln1_gain, ("seq", "head"), axis=0, tiled=True),
        lax.all_gather(ln1_bias, ("seq", "head"), axis=0, tiled=True),
        lax.all_gather(w_out, ("seq", "head"), axis=0, tiled=True),
        lax.all_gather(b_out, ("seq", "head"), axis=0, tiled=True),
        lax.all_gather(ln2_gain, ("seq", "head"), axis=0, tiled=True),
        lax.all_gather(ln2_bias, ("seq", "head"), axis=0, tiled=True),
        lax.all_gather(w_up, ("seq", "head"), axis=1, tiled=True),
        lax.all_gather(b_up, ("seq", "head"), axis=0, tiled=True),
        lax.all_gather(w_down, ("seq", "head"), axis=0, tiled=True),
        lax.all_gather(b_down, ("seq", "head"), axis=0, tiled=True),
    )
    gain_one = gathered[0].astype(FLOAT)
    shift_one = gathered[1].astype(FLOAT)
    proj_out = gathered[2]
    bias_out = gathered[3].astype(FLOAT)
    gain_two = gathered[4].astype(FLOAT)
    shift_two = gathered[5].astype(FLOAT)
    proj_up = gathered[6]
    bias_up = gathered[7].astype(FLOAT)
    proj_down = gathered[8]
    bias_down = gathered[9].astype(FLOAT)
    inputs_f = layer_input.astype(FLOAT)
    normed_one = layer_norm(inputs_f, gain_one, shift_one).astype(LOWER)
    joined_w = jnp.concatenate([w_query, w_key, w_value], axis=1)
    bias_row = jnp.concatenate([b_query, jnp.zeros_like(b_query), b_value]).astype(FLOAT)
    scale_row = jnp.concatenate(
        [jnp.full((local_width,), scale, FLOAT), jnp.ones((2 * local_width,), FLOAT)]
    )
    packed = (
        (
            jnp.dot(
                lax.all_gather(normed_one, "head", axis=0, tiled=True),
                joined_w,
                preferred_element_type=FLOAT,
            )
            + bias_row
        )
        * scale_row
    ).astype(LOWER)
    query = packed[:, :local_width]
    keys = packed[:, local_width : 2 * local_width]
    values = packed[:, 2 * local_width :]
    group_rows = query.shape[0]
    heads_shape = (group_rows, local_heads, HEAD_DIM)
    query_heads = query.reshape(heads_shape)
    keys_heads = keys.reshape(heads_shape)
    values_heads = values.reshape(heads_shape)
    context, logsum = attention_forward(
        query_heads, keys_heads, values_heads, mem_count, text_len, slot_count
    )
    ctx_tok = lax.all_to_all(
        context.reshape(group_rows, local_width), "head", split_axis=0, concat_axis=1, tiled=True
    )
    attended = jnp.dot(ctx_tok, proj_out, preferred_element_type=FLOAT) + bias_out
    hidden = inputs_f + attended
    normed_two = layer_norm(hidden, gain_two, shift_two).astype(LOWER)
    grad_out_f = cotangent.astype(FLOAT)
    grad_b_down = jnp.sum(grad_out_f, 0)
    pre_act = jnp.dot(normed_two, proj_up, preferred_element_type=FLOAT) + bias_up
    act_full, gelu_back = jax.vjp(exact_gelu, pre_act)
    activated = act_full.astype(LOWER)
    output = (
        hidden + (jnp.dot(activated, proj_down, preferred_element_type=FLOAT) + bias_down)
    ).astype(LOWER)
    grad_w_down = contract_rows(activated, cotangent)
    (grad_pre,) = gelu_back(contract_cols(cotangent, proj_down))
    grad_pre_low = grad_pre.astype(LOWER)
    grad_w_up = contract_rows(normed_two, grad_pre_low)
    grad_b_up = jnp.sum(grad_pre_low.astype(FLOAT), 0)
    grad_normed_two = contract_cols(grad_pre_low, proj_up)
    _, norm_two_back = jax.vjp(layer_norm, hidden, gain_two, shift_two)
    grad_from_norm, grad_gain_two, grad_shift_two = norm_two_back(grad_normed_two)
    grad_hidden = grad_out_f + grad_from_norm
    grad_att = grad_hidden.astype(LOWER)
    grad_w_out = contract_rows(ctx_tok, grad_att)
    grad_b_out = jnp.sum(grad_att.astype(FLOAT), 0)
    grad_ctx = contract_cols(grad_att, proj_out).astype(LOWER)
    grad_ctx_heads = lax.all_to_all(
        grad_ctx, "head", split_axis=1, concat_axis=0, tiled=True
    ).reshape(heads_shape)
    grad_query, grad_keys, grad_values = attention_backward(
        query_heads,
        keys_heads,
        values_heads,
        grad_ctx_heads,
        logsum,
        mem_count,
        text_len,
        slot_count,
    )
    grad_q_low = (grad_query.astype(LOWER) * scale).reshape(group_rows, local_width)
    grad_k_low = grad_keys.astype(LOWER).reshape(group_rows, local_width)
    grad_v_low = grad_values.astype(LOWER).reshape(group_rows, local_width)
    grad_joined = jnp.concatenate([grad_q_low, grad_k_low, grad_v_low], axis=1)
    rows_here = grad_joined
    joined_grad = contract_rows(lax.all_gather(normed_one, "head", axis=0, tiled=True), rows_here)
    weight_part = jnp.stack(
        [
            joined_grad[:, :local_width],
            joined_grad[:, local_width : 2 * local_width],
            joined_grad[:, 2 * local_width :],
        ]
    )
    bias_part = jnp.stack(
        [jnp.sum(grad_q_low.astype(FLOAT), 0), jnp.sum(grad_v_low.astype(FLOAT), 0)]
    )
    rows_here = grad_joined
    grad_normed = lax.psum_scatter(
        contract_cols(rows_here, joined_w).astype(jnp.bfloat16),
        "head",
        scatter_dimension=0,
        tiled=True,
    ).astype(jnp.float32)
    weight_sum, bias_sum = (
        lax.psum(weight_part.astype(jnp.bfloat16), "seq").astype(jnp.float32),
        lax.psum(bias_part.astype(jnp.bfloat16), "seq").astype(jnp.float32),
    )
    _, norm_one_back = jax.vjp(layer_norm, inputs_f, gain_one, shift_one)
    grad_in_norm, grad_gain_one, grad_shift_one = norm_one_back(grad_normed)
    grad_input = (grad_hidden + grad_in_norm).astype(LOWER)
    scattered = (
        lax.psum_scatter(grad_gain_one, ("seq", "head"), scatter_dimension=0, tiled=True),
        lax.psum_scatter(grad_shift_one, ("seq", "head"), scatter_dimension=0, tiled=True),
        lax.psum_scatter(grad_w_out, ("seq", "head"), scatter_dimension=0, tiled=True),
        lax.psum_scatter(grad_b_out, ("seq", "head"), scatter_dimension=0, tiled=True),
        lax.psum_scatter(grad_gain_two, ("seq", "head"), scatter_dimension=0, tiled=True),
        lax.psum_scatter(grad_shift_two, ("seq", "head"), scatter_dimension=0, tiled=True),
        lax.psum_scatter(grad_w_up, ("seq", "head"), scatter_dimension=1, tiled=True),
        lax.psum_scatter(grad_b_up, ("seq", "head"), scatter_dimension=0, tiled=True),
        lax.psum_scatter(grad_w_down, ("seq", "head"), scatter_dimension=0, tiled=True),
        lax.psum_scatter(grad_b_down, ("seq", "head"), scatter_dimension=0, tiled=True),
    )
    return (
        output,
        grad_input,
        weight_sum[0],
        weight_sum[1],
        weight_sum[2],
        bias_sum[0],
        bias_sum[1],
        scattered[0],
        scattered[1],
        scattered[2],
        scattered[3],
        scattered[4],
        scattered[5],
        scattered[6],
        scattered[7],
        scattered[8],
        scattered[9],
    )


def solution(mesh):
    return jax.shard_map(
        body,
        mesh=mesh,
        in_specs=(
            P(("seq", "head"), None),
            P("seq"),
            P("seq"),
            P("seq"),
            P(None, "head"),
            P(None, "head"),
            P(None, "head"),
            P("head"),
            P("head"),
            P(("seq", "head")),
            P(("seq", "head")),
            P(("seq", "head"), None),
            P(("seq", "head")),
            P(("seq", "head")),
            P(("seq", "head")),
            P(None, ("seq", "head")),
            P(("seq", "head")),
            P(("seq", "head"), None),
            P(("seq", "head")),
            P(("seq", "head"), None),
        ),
        out_specs=(
            P(("seq", "head"), None),
            P(("seq", "head"), None),
            P(None, "head"),
            P(None, "head"),
            P(None, "head"),
            P("head"),
            P("head"),
            P(("seq", "head")),
            P(("seq", "head")),
            P(("seq", "head"), None),
            P(("seq", "head")),
            P(("seq", "head")),
            P(("seq", "head")),
            P(None, ("seq", "head")),
            P(("seq", "head")),
            P(("seq", "head"), None),
            P(("seq", "head")),
        ),
        check_vma=False,
    )
```

profile of v0, /device:TPU:0, one launch (start us, length us, event | category | flops | bytes accessed | tf_op | source)
XLA Modules:
  0.0 2882.2 jit_solution(14539139837543407453)
XLA Ops:
  12.5 42.5 %all-reduce.14 = (bf16[2048]{0:T(1024)(128)(2,1)S(1)}, bf16[2048]{0:T(1024)(128)(2,1)S(1)}, bf16[2048]{0:T(1024)(128)(2,1)}, bf16[2048]{0:T(1024)(128)(2,1)}, bf...) all-reduce(bf16[2048]{0:T(1024)(128)(2,1)S(1)} %dynamic-update-slic, ...), channel_id=1, replica_groups=mesh['seq'=4,'head'=8] {'seq','head'}, use_global_device_ids=true, to_apply=%add.1 | all-reduce | flops 12288 | bytes 49152
  69.5 75.0 %all-gather.6.cloned.1.call-done = bf16[2048,2048]{1,0:T(8,128)(2,1)} async-done(((bf16[256,2048]{1,0:T(8,128)(2,1)}), bf16[2048,2048]{1,0:T(8,128)(2,1)}) %all-gather.6.cloned.1.call-update) | async-done | bytes 8388624 | tf_op jit(solution)/shard_map/all_gather | solution.py:170
  144.5 10.2 multiply_convert_fusion.2
  156.0 77.7 %while.31 = (s32[]{:T(128)}, bf16[4,512,4,64]{1,3,2,0:T(8,128)(2,1)}, f32[4,4,512]{2,1,0:T(4,128)}, s32[]{:T(128)}, s32[]{:T(128)}, /*index=5*/s32[4]{0:T(128)S(...) while((s32[]{:T(128)}, ...), condition=%wide.region_5.6_spmd, body=%wide.region_2.5_spmd.sunk | while | flops 1116871168 | bytes 57225684 | solution.py:74
  169.2 5.6 fusion.128
  188.6 5.6 fusion.128
  208.1 5.6 fusion.128
  227.5 5.6 fusion.128
  245.9 66.5 %all-gather = bf16[32,1,256]{2,1,0:T(2,128)(2,1)S(1)} all-gather(bf16[1,1,256]{2,1,0:T(2,128)(2,1)S(1)} %reshape.341), channel_id=1, replica_groups=mesh['seq'=4,'head'=8] {'seq','head'}, dimensions={0}, use_global_device_ids=true | all-gather | bytes 16896 | tf_op jit(solution)/shard_map/all_gather | solution.py:146
  312.6 6.2 fusion.75
  320.4 110.7 %all-gather.10.cloned.1.call-done = bf16[2048,8192]{1,0:T(8,128)(2,1)} async-done(((bf16[2048,256]{1,0:T(8,128)(2,1)}), bf16[2048,8192]{1,0:T(8,128)(2,1)}) %all-gather.10.cloned.1.call-update) | async-done | bytes 33554448 | tf_op jit(solution)/shard_map/all_gather | solution.py:145
  431.1 18.4 convolution_add_fusion
  449.5 178.8 %all-gather.12.cloned.1.call-done = bf16[8192,2048]{1,0:T(8,128)(2,1)} async-done(((bf16[256,2048]{1,0:T(8,128)(2,1)}), bf16[8192,2048]{1,0:T(8,128)(2,1)}) %all-gather.12.cloned.1.call-update) | async-done | bytes 33554448 | tf_op jit(solution)/shard_map/all_gather | solution.py:147
  628.3 34.2 %convert_reduce_fusion = (f32[8192]{0:T(1024)}, bf16[256,8192]{1,0:T(8,128)(2,1)}, f32[256,8192]{1,0:T(8,128)}) fusion(f32[256,8192]{1,0:T(8,128)} %convolution_add_fusion, bf16[256,2048]{1,0:T(8,128)(2,1)S(1)} %copy-done.13, bf16[8192,2048]{1,0:T(8,128)(2,1)} %all-gather.12.cloned.1.call-done), kind=kOutput, calls=%fused_computation.62 | convolution fusion | flops 8745115648 | bytes 55607296 | tf_op jit(solution)/shard_map/dot_general | solution.py:40
  662.5 18.8 multiply_reduce_fusion.1
  686.5 6.1 convolution_convert_fusion.2
  697.4 26.4 all-to-all-done.1
  727.9 213.0 %while.32 = (s32[]{:T(128)}, f32[2048,4,64]{0,2,1:T(8,128)}, f32[2048,4,64]{0,2,1:T(8,128)}, bf16[4,512,4,64]{1,3,2,0:T(8,128)(2,1)}, s32[4]{0:T(128)S(1)}, /*in...) while((s32[]{:T(128)}, f32[2048,4,64]{0,2,1:T(8,128)}, ...), condition=%wide.region_12.13_spmd.clone, body=%wide.region_10.12_spmd.clone.sunk | while | flops 2742032896 | bytes 277418816 | solution.py:107
  737.8 11.9 multiply_reduce_fusion.5
  749.7 10.6 multiply_convert_fusion.4
  760.3 6.5 fusion.140
  766.9 8.2 fusion.141
  775.1 4.7 fusion.142
  790.6 11.9 multiply_reduce_fusion.5
  802.4 10.6 multiply_convert_fusion.4
  813.1 7.1 fusion.140
  820.2 8.2 fusion.141
  843.9 11.9 multiply_reduce_fusion.5
  855.7 10.6 multiply_convert_fusion.4
  866.4 7.1 fusion.140
  873.5 8.2 fusion.141
  897.2 11.9 multiply_reduce_fusion.5
  909.0 10.6 multiply_convert_fusion.4
  919.7 7.1 fusion.140
  926.8 8.2 fusion.141
  947.1 10.8 convolution_convert_fusion
  958.0 9.2 convolution_convert_fusion.1
  970.0 75.6 %reduce-scatter.5.cloned.1.call-done = bf16[256,2048]{1,0:T(8,128)(2,1)} async-done(((bf16[2048,2048]{1,0:T(8,128)(2,1)}), bf16[256,2048]{1,0:T(8,128)(2,1)}) %reduce-scatter.5.cloned.1.call-update) | async-done | bytes 1048592 | tf_op jit(solution)/shard_map/reduce_scatter | solution.py:246
  1055.8 9.7 fusion.76
  1067.0 26.4 fusion.67
  1093.7 10.2 multiply_convert_fusion.1
  1103.9 26.9 fusion.77
  1131.4 17.0 fusion.53
  1148.7 9.3 psum.15
  1163.9 101.7 %all-reduce.20.cloned.1.call-done = (f32[2048]{0:T(1024)}, f32[2048]{0:T(1024)}, f32[2048]{0:T(1024)}, f32[2048]{0:T(1024)}, f32[2048]{0:T(1024)}, /*index=5*/f32[8192]{0:T(1024)}, f32[2048]{0:T(1024)}) async-done(((f32[2048]{0:T(1024)}, f32[2048]{0:T(1024)}, f32[2048]{0:T(1024)}, f32[2048]{0:T(1024)}, f32[2048]{0:T(1024)}, /*index=5*/f32[8192]{0:T(1024)}, f32[2048]{0:T(1024)}), (f32[2048]{0:T(1024)}, ...) | async-done | bytes 81936
  1274.4 181.9 %reduce-scatter.7.cloned.1.call-done = f32[64,2048]{1,0:T(8,128)} async-done(((f32[2048,2048]{1,0:T(8,128)}), f32[64,2048]{1,0:T(8,128)}) %reduce-scatter.7.cloned.1.call-update) | async-done | bytes 524304 | tf_op jit(solution)/shard_map/reduce_scatter | solution.py:262
  1456.4 710.0 %reduce-scatter.9.cloned.1.call-done = f32[2048,256]{1,0:T(8,128)} async-done(((f32[2048,8192]{1,0:T(8,128)}), f32[2048,256]{1,0:T(8,128)}) %reduce-scatter.9.cloned.1.call-update) | async-done | bytes 2097168 | tf_op jit(solution)/shard_map/reduce_scatter | solution.py:266
  2166.4 708.7 %reduce-scatter.11.cloned.1.call-done = f32[256,2048]{1,0:T(8,128)} async-done(((f32[8192,2048]{1,0:T(8,128)}), f32[256,2048]{1,0:T(8,128)}) %reduce-scatter.11.cloned.1.call-update) | async-done | bytes 2097168 | tf_op jit(solution)/shard_map/reduce_scatter | solution.py:268
  (330 shorter events, 173.9 us)
Async XLA Ops:
  7.2 58.9 %copy-start.46 = (bf16[256]{0:T(256)(128)(2,1)S(1)}, bf16[256]{0:T(256)(128)(2,1)}, u32[]{:S(2)}) copy-start(bf16[256]{0:T(256)(128)(2,1)} %param.32) | copy-start | bytes 1540
  7.2 58.9 %copy-start.47 = (bf16[256]{0:T(256)(128)(2,1)S(1)}, bf16[256]{0:T(256)(128)(2,1)}, u32[]{:S(2)}) copy-start(bf16[256]{0:T(256)(128)(2,1)} %param.31) | copy-start | bytes 1540
  7.2 58.9 %copy-start.16 = (bf16[2048,256]{1,0:T(8,128)(2,1)S(1)}, bf16[2048,256]{1,0:T(8,128)(2,1)}, u32[]{:S(2)}) copy-start(bf16[2048,256]{1,0:T(8,128)(2,1)} %param.28) | copy-start | bytes 3145732
  7.2 60.0 %copy-start.17 = (bf16[2048,256]{1,0:T(8,128)(2,1)S(1)}, bf16[2048,256]{1,0:T(8,128)(2,1)}, u32[]{:S(2)}) copy-start(bf16[2048,256]{1,0:T(8,128)(2,1)} %param.29) | copy-start | bytes 3145732
  7.2 61.1 %copy-start.18 = (bf16[2048,256]{1,0:T(8,128)(2,1)S(1)}, bf16[2048,256]{1,0:T(8,128)(2,1)}, u32[]{:S(2)}) copy-start(bf16[2048,256]{1,0:T(8,128)(2,1)} %param.30) | copy-start | bytes 3145732
  7.2 137.3 %all-gather.6.cloned.1.call-start = ((), (), s32[]{:S(2)}) async-start(), calls=%async_computation.6 | async-start | bytes 9437184 | tf_op jit(solution)/shard_map/all_gather | solution.py:170
  56.6 88.0 %copy-start.49 = (f32[768]{0:T(1024)S(1)}, f32[768]{0:T(1024)}, u32[]{:S(2)}) copy-start(f32[768]{0:T(1024)} %constant.211.clone.1) | copy-start | bytes 9220
  62.1 250.5 %all-gather.8.cloned.1.call-start = ((), (), s32[]{:S(2)}) async-start(), calls=%async_computation.7 | async-start | bytes 8650752 | tf_op jit(solution)/shard_map/all_gather | solution.py:141
  62.8 368.3 %all-gather.10.cloned.1.call-start = ((), (), s32[]{:S(2)}) async-start(), calls=%async_computation.8 | async-start | bytes 34603008 | tf_op jit(solution)/shard_map/all_gather | solution.py:145
  63.6 564.7 %all-gather.12.cloned.1.call-start = ((), (), s32[]{:S(2)}) async-start(), calls=%async_computation.9 | async-start | bytes 34603008 | tf_op jit(solution)/shard_map/all_gather | solution.py:147
  233.7 12.1 copy-start.45
  233.7 12.2 copy-start.48
  233.7 78.7 %copy-start.44 = (bf16[2048]{0:T(1024)(128)(2,1)S(1)}, bf16[2048]{0:T(1024)(128)(2,1)}, u32[]{:S(2)}) copy-start(bf16[2048]{0:T(1024)(128)(2,1)} %get-tuple-element.445) | copy-start | bytes 12292
  233.7 78.7 %copy-start.43 = (bf16[2048]{0:T(1024)(128)(2,1)S(1)}, bf16[2048]{0:T(1024)(128)(2,1)}, u32[]{:S(2)}) copy-start(bf16[2048]{0:T(1024)(128)(2,1)} %get-tuple-element.446) | copy-start | bytes 12292
  233.7 78.8 %copy-start.5 = (bf16[256,2048]{1,0:T(8,128)(2,1)S(1)}, bf16[256,2048]{1,0:T(8,128)(2,1)}, u32[]{:S(2)}) copy-start(bf16[256,2048]{1,0:T(8,128)(2,1)} %param.24) | copy-start | bytes 3145732
  241.4 71.1 %all-to-all-start = ((bf16[8,256,256]{1,2,0:T(8,128)(2,1)}), bf16[8,256,256]{1,2,0:T(8,128)(2,1)}, u32[]{:S(2)}, u32[]{:S(2)}) async-start(bf16[8,256,256]{1,2,0:T(8,128)(2,1)} %copy.48), calls=%async_computation | async-start | bytes 2097152 | tf_op jit(solution)/shard_map/all_to_all | solution.py:189
  312.5 118.6 %copy-start.24 = (f32[2048]{0:T(1024)}, f32[2048]{0:T(1024)S(1)}, u32[]{:S(2)}) copy-start(f32[2048]{0:T(1024)S(1)} %convert_element_type.136) | copy-start | bytes 24580
  312.5 368.8 %copy-start.22 = (f32[2048]{0:T(1024)}, f32[2048]{0:T(1024)S(1)}, u32[]{:S(2)}) copy-start(f32[2048]{0:T(1024)S(1)} %convert_element_type.135) | copy-start | bytes 24580
  318.8 362.6 %copy-start.28 = (f32[256]{0:T(256)}, f32[256]{0:T(256)S(1)}, u32[]{:S(2)}) copy-start(f32[256]{0:T(256)S(1)} %broadcast_multiply_fusion) | copy-start | bytes 3076
  320.4 360.9 %copy-start.30 = (f32[256]{0:T(256)}, f32[256]{0:T(256)S(1)}, u32[]{:S(2)}) copy-start(f32[256]{0:T(256)S(1)} %fusion.64) | copy-start | bytes 3076
  431.1 197.2 %copy-start.13 = (bf16[256,2048]{1,0:T(8,128)(2,1)S(1)}, bf16[256,2048]{1,0:T(8,128)(2,1)}, u32[]{:S(2)}) copy-start(bf16[256,2048]{1,0:T(8,128)(2,1)} %param.43) | copy-start | bytes 3145732
  684.2 8.4 copy-start.36
  693.7 30.1 %all-to-all-start.1 = ((bf16[256,8,256]{2,0,1:T(8,128)(2,1)}), bf16[256,8,256]{2,0,1:T(8,128)(2,1)S(1)}, u32[]{:S(2)}, u32[]{:S(2)}) async-start(bf16[256,8,256]{2,0,1:T(8,128)(2,1)} %bitcast.134), calls=%async_computation.1 | async-start | bytes 2097152 | tf_op jit(solution)/shard_map/all_to_all | solution.py:216
  697.3 348.4 %reduce-scatter.5.cloned.1.call-start = ((), (), s32[]{:S(2)}) async-start(), calls=%async_computation.10 | async-start | bytes 9437184 | tf_op jit(solution)/shard_map/reduce_scatter | solution.py:246
  734.8 14.9 copy-start
  760.3 14.8 slice-start
  787.5 14.9 copy-start
  813.1 15.4 slice-start
  820.2 8.3 copy-start.19
  840.8 14.9 copy-start
  866.4 15.4 slice-start
  894.1 14.9 copy-start
  919.7 15.4 slice-start
  958.0 200.6 %all-reduce.18.cloned.1.call-start = ((), (), s32[]{:S(2)}) async-start(), calls=%async_computation.11 | async-start | bytes 6291456 | tf_op jit(solution)/shard_map/psum | solution.py:253
  967.4 78.2 %copy-start.6 = (bf16[256,2048]{1,0:T(8,128)(2,1)S(1)}, bf16[256,2048]{1,0:T(8,128)(2,1)}, u32[]{:S(2)}) copy-start(bf16[256,2048]{1,0:T(8,128)(2,1)} %param.24) | copy-start | bytes 3145732
  967.5 78.2 %copy-start.27 = (f32[2048]{0:T(1024)S(1)}, f32[2048]{0:T(1024)}, u32[]{:S(2)}) copy-start(f32[2048]{0:T(1024)} %copy-done.26) | copy-start | bytes 24580
  967.5 78.2 %copy-start.33 = (f32[256]{0:T(256)S(1)}, f32[256]{0:T(256)}, u32[]{:S(2)}) copy-start(f32[256]{0:T(256)} %copy-done.32) | copy-start | bytes 3076
  967.5 80.7 %copy-start.39 = (f32[256]{0:T(256)S(1)}, f32[256]{0:T(256)}, u32[]{:S(2)}) copy-start(f32[256]{0:T(256)} %copy-done.38) | copy-start | bytes 3076
  967.5 80.7 %copy-start.35 = (f32[256]{0:T(256)S(1)}, f32[256]{0:T(256)}, u32[]{:S(2)}) copy-start(f32[256]{0:T(256)} %copy-done.34) | copy-start | bytes 3076
  967.5 83.6 %copy-start.12 = (f32[256,2048]{1,0:T(8,128)S(1)}, f32[256,2048]{1,0:T(8,128)}, u32[]{:S(2)}) copy-start(f32[256,2048]{1,0:T(8,128)} %copy-done.11) | copy-start | bytes 6291460
  967.5 83.6 %copy-start.37 = (f32[256]{0:T(256)S(1)}, f32[256]{0:T(256)}, u32[]{:S(2)}) copy-start(f32[256]{0:T(256)} %copy-done.36) | copy-start | bytes 3076
  969.6 296.0 %all-reduce.20.cloned.1.call-start = ((), (), s32[]{:S(2)}) async-start(), calls=%async_computation.15 | async-start | bytes 163840
  1055.7 400.7 %reduce-scatter.7.cloned.1.call-start = ((), (), s32[]{:S(2)}) async-start(), calls=%async_computation.12 | async-start | bytes 17301504 | tf_op jit(solution)/shard_map/reduce_scatter | solution.py:262
  1065.5 1100.9 %reduce-scatter.9.cloned.1.call-start = ((), (), s32[]{:S(2)}) async-start(), calls=%async_computation.13 | async-start | bytes 69206016 | tf_op jit(solution)/shard_map/reduce_scatter | solution.py:266
  1093.5 1781.7 %reduce-scatter.11.cloned.1.call-start = ((), (), s32[]{:S(2)}) async-start(), calls=%async_computation.14 | async-start | bytes 69206016 | tf_op jit(solution)/shard_map/reduce_scatter | solution.py:268
  1093.7 10.2 copy-start.14
  1131.4 17.1 copy-start.40
  1131.4 17.1 copy-start.41
  (49 other events, 223.2 us)
Sparse Core Ops, SparseCore 0:
  62.2 82.2 all-gather.5
  147.5 75.9 all-gather.7
  225.0 206.0 all-gather.9
  433.9 194.2 all-gather.11
  958.1 87.5 reduce-scatter.4
  1048.6 85.5 all-reduce.17
  1141.7 123.7 all-reduce.19
  1268.4 187.9 reduce-scatter.6
  1459.3 707.0 reduce-scatter.8
  2169.2 705.9 reduce-scatter.10
where the time goes:
time: 2890 us; the launch traced here: 2880 us
  waiting for transfers between devices  2170 us (75%)
  matrix products  372 us (13%)
  other arithmetic  119 us (4%)
  blocking collectives  118 us (4%)
  local copies, waits for them, and re-layouts  54.4 us (2%)
    reduce_scatter x1, waiting for transfers between devices, body(): lax.psum_scatter(grad_w_up, ('seq', 'head'), scatter_dimension=1, tiled=T...  710 us
    reduce_scatter x1, waiting for transfers between devices, body(): lax.psum_scatter(grad_w_down, ('seq', 'head'), scatter_dimension=0, tiled...  709 us
    reduce_scatter x1, waiting for transfers between devices, body(): lax.psum_scatter(grad_w_out, ('seq', 'head'), scatter_dimension=0, tiled=...  182 us
    all_gather x1, waiting for transfers between devices, body(): lax.all_gather(w_down, ('seq', 'head'), axis=0, tiled=True)  179 us
    all_gather x1, waiting for transfers between devices, body(): lax.all_gather(w_up, ('seq', 'head'), axis=1, tiled=True)  111 us
    unnamed x11, waiting for transfers between devices  104 us
    reduce_scatter x1, waiting for transfers between devices, body(): lax.psum_scatter(contract_cols(rows_here, joined_w).astype(jnp.bfloat16),...  75.6 us
    all_gather x1, waiting for transfers between devices, body(): lax.all_gather(normed_one, 'head', axis=0, tiled=True)  75 us
  transfers between devices with their start and end apart: 12, of which 9 were waited for; matrix products, arithmetic and copies ran while one was open for 8% of the time, Pallas kernels for 0%

commit v1 on v0

v1 whole, which is shorter than its diff:
```python
import functools

import jax
import jax.numpy as jnp
from jax import lax
from jax.experimental import pallas as pl
from jax.experimental.pallas import tpu as pltpu
from jax.sharding import PartitionSpec as P

HEAD_DIM = 64
LENGTH = 2048
NEG = -1e30
FLOAT = jnp.float32
LOWER = jnp.bfloat16
BLOCK = 512


def cols_by_cols(left, right):
    return lax.dot_general(left, right, (((1,), (1,)), ((), ())), preferred_element_type=FLOAT)


def key_bias(key_first, query_first, rows, cols, memory, text_count, slot_num, diagonal):
    key_pos = key_first + lax.broadcasted_iota(jnp.int32, (rows, 1), 0)
    valid = (key_pos < memory + text_count) | (key_pos >= LENGTH - slot_num)
    if not diagonal:
        return jnp.where(valid, 0.0, NEG)
    first_bias = jnp.where(valid, 0.0, NEG)
    mem_bias = jnp.where(key_pos < memory, 0.0, NEG)
    key_grid = key_first + lax.broadcasted_iota(jnp.int32, (rows, cols), 0)
    query_grid = query_first + lax.broadcasted_iota(jnp.int32, (rows, cols), 1)
    bias = jnp.where(key_grid < query_grid, 0.0, mem_bias) + first_bias
    return jnp.where(key_grid == query_grid, 0.0, jnp.maximum(bias, NEG))


def forward_kernel(count_ref, q_ref, k_ref, v_ref, out_ref, out32_ref, lse_ref, v_t, acc, stat):
    width = q_ref.shape[1]
    heads = width // HEAD_DIM
    seq = pl.program_id(0)
    block = pl.program_id(1)

    @pl.when(block == 0)
    def _():
        v_t[...] = v_ref[...].astype(FLOAT).T.astype(LOWER)

    memory, text_count, slot_num = count_ref[0, seq], count_ref[1, seq], count_ref[2, seq]
    query = q_ref[...]
    lane_head = lax.broadcasted_iota(jnp.int32, query.shape, 1) // HEAD_DIM
    zero = jnp.zeros_like(query)
    parts = [jnp.where(lane_head == h, query, zero) for h in range(heads)]

    def chunk(key_block, diagonal):
        first = pl.multiple_of(key_block * BLOCK, BLOCK)
        keys = k_ref[pl.ds(first, BLOCK), :]
        bias = key_bias(first, block * BLOCK, BLOCK, BLOCK, memory, text_count, slot_num, diagonal)
        for h in range(heads):
            rows = slice(h * HEAD_DIM, (h + 1) * HEAD_DIM)
            scores = cols_by_cols(keys, parts[h]) + bias
            top = jnp.max(scores, axis=0, keepdims=True)
            if not diagonal:
                old = stat[h : h + 1, :]
                top = jnp.maximum(top, old)
            expo = jnp.exp(scores - top)
            total = jnp.sum(expo, axis=0, keepdims=True)
            mixed = jnp.dot(
                v_t[rows, pl.ds(first, BLOCK)], expo.astype(LOWER), preferred_element_type=FLOAT
            )
            if diagonal:
                stat[heads + h : heads + h + 1, :] = total
                acc[rows, :] = mixed
            else:
                shrink = jnp.exp(old - top)
                stat[heads + h : heads + h + 1, :] = stat[heads + h : heads + h + 1, :] * shrink + total
                acc[rows, :] = acc[rows, :] * shrink + mixed
            stat[h : h + 1, :] = top

    chunk(block, True)

    @pl.loop(0, block)
    def _(key_block):
        chunk(key_block, False)

    for h in range(heads):
        rows = slice(h * HEAD_DIM, (h + 1) * HEAD_DIM)
        total = stat[heads + h : heads + h + 1, :]
        acc[rows, :] = acc[rows, :] / total
        lse_ref[h : h + 1, :] = stat[h : h + 1, :] + jnp.log(total)
    flat = acc[...].T
    out32_ref[...] = flat
    out_ref[...] = flat.astype(LOWER)


def attention_forward(query, keys, values, counts):
    rows, width = query.shape
    seqs, blocks = rows // LENGTH, LENGTH // BLOCK
    by_block = pl.BlockSpec((BLOCK, width), lambda s, b, c: (s * blocks + b, 0))
    by_seq = pl.BlockSpec((LENGTH, width), lambda s, b, c: (s, 0))
    heads = width // HEAD_DIM
    return pl.pallas_call(
        forward_kernel,
        grid_spec=pltpu.PrefetchScalarGridSpec(
            num_scalar_prefetch=1,
            grid=(seqs, blocks),
            in_specs=[by_block, by_seq, by_seq],
            out_specs=[
                by_block,
                by_block,
                pl.BlockSpec((8, BLOCK), lambda s, b, c: (0, s * blocks + b)),
            ],
            scratch_shapes=[
                pltpu.VMEM((width, LENGTH), LOWER),
                pltpu.VMEM((width, BLOCK), FLOAT),
                pltpu.VMEM((2 * heads, BLOCK), FLOAT),
            ],
        ),
        out_shape=[
            jax.ShapeDtypeStruct((rows, width), LOWER),
            jax.ShapeDtypeStruct((rows, width), FLOAT),
            jax.ShapeDtypeStruct((8, rows), FLOAT),
        ],
        compiler_params=pltpu.CompilerParams(vmem_limit_bytes=48 * 2**20),
        name="attn_fwd",
    )(counts, query, keys, values)


def backward_kernel(
    count_ref, q_ref, k_ref, v_ref, o_ref, do_ref, lse_ref, dq_ref, dk_ref, dv_ref, dq_t, delta, k_t, dk_acc, dv_acc
):
    width = q_ref.shape[1]
    heads = width // HEAD_DIM
    seq = pl.program_id(0)
    block = pl.program_id(1)
    blocks = LENGTH // BLOCK

    @pl.when(block == 0)
    def _():
        dq_t[...] = jnp.zeros_like(dq_t)
        for b in range(blocks):
            span = slice(b * BLOCK, (b + 1) * BLOCK)
            flipped = (do_ref[span, :].astype(FLOAT) * o_ref[span, :]).T
            for h in range(heads):
                rows = slice(h * HEAD_DIM, (h + 1) * HEAD_DIM)
                delta[h : h + 1, span] = jnp.sum(flipped[rows, :], axis=0, keepdims=True)

    memory, text_count, slot_num = count_ref[0, seq], count_ref[1, seq], count_ref[2, seq]
    keys = k_ref[...]
    values = v_ref[...]
    k_t[...] = keys.astype(FLOAT).T.astype(LOWER)
    lane_head = lax.broadcasted_iota(jnp.int32, (BLOCK, width), 1) // HEAD_DIM

    def chunk(query_block, diagonal):
        first = pl.multiple_of(query_block * BLOCK, BLOCK)
        span = pl.ds(first, BLOCK)
        query = q_ref[span, :]
        grad = do_ref[span, :]
        zero = jnp.zeros_like(query)
        bias = key_bias(block * BLOCK, first, BLOCK, BLOCK, memory, text_count, slot_num, diagonal)
        for h in range(heads):
            rows = slice(h * HEAD_DIM, (h + 1) * HEAD_DIM)
            q_part = jnp.where(lane_head == h, query, zero)
            g_part = jnp.where(lane_head == h, grad, zero)
            scores = cols_by_cols(keys, q_part) + bias
            probs = jnp.exp(scores - lse_ref[h : h + 1, span])
            grad_probs = cols_by_cols(values, g_part)
            grad_scores = (probs * (grad_probs - delta[h : h + 1, span])).astype(LOWER)
            part_v = jnp.dot(probs.astype(LOWER), g_part, preferred_element_type=FLOAT)
            part_k = jnp.dot(grad_scores, q_part, preferred_element_type=FLOAT)
            if diagonal and h == 0:
                dv_acc[...] = part_v
                dk_acc[...] = part_k
            else:
                dv_acc[...] += part_v
                dk_acc[...] += part_k
            dq_t[rows, span] += jnp.dot(k_t[rows, :], grad_scores, preferred_element_type=FLOAT)

    chunk(block, True)

    @pl.loop(block + 1, blocks)
    def _(query_block):
        chunk(query_block, False)

    dk_ref[...] = dk_acc[...].astype(LOWER)
    dv_ref[...] = dv_acc[...].astype(LOWER)

    @pl.when(block == blocks - 1)
    def _():
        scale = HEAD_DIM ** (-0.5)
        for b in range(blocks):
            span = slice(b * BLOCK, (b + 1) * BLOCK)
            dq_ref[span, :] = (dq_t[:, span].T.astype(LOWER) * scale).astype(LOWER)


def attention_backward(query, keys, values, out32, grad, lse, counts):
    rows, width = query.shape
    seqs, blocks = rows // LENGTH, LENGTH // BLOCK
    by_block = pl.BlockSpec((BLOCK, width), lambda s, b, c: (s * blocks + b, 0))
    by_seq = pl.BlockSpec((LENGTH, width), lambda s, b, c: (s, 0))
    return pl.pallas_call(
        backward_kernel,
        grid_spec=pltpu.PrefetchScalarGridSpec(
            num_scalar_prefetch=1,
            grid=(seqs, blocks),
            in_specs=[
                by_seq,
                by_block,
                by_block,
                by_seq,
                by_seq,
                pl.BlockSpec((8, LENGTH), lambda s, b, c: (0, s)),
            ],
            out_specs=[by_seq, by_block, by_block],
            scratch_shapes=[
                pltpu.VMEM((width, LENGTH), FLOAT),
                pltpu.VMEM((8, LENGTH), FLOAT),
                pltpu.VMEM((width, BLOCK), LOWER),
                pltpu.VMEM((BLOCK, width), FLOAT),
                pltpu.VMEM((BLOCK, width), FLOAT),
            ],
        ),
        out_shape=[jax.ShapeDtypeStruct((rows, width), LOWER)] * 3,
        compiler_params=pltpu.CompilerParams(vmem_limit_bytes=48 * 2**20),
        name="attn_bwd",
    )(counts, query, keys, values, out32, grad, lse)


EPS = 1e-05


def layer_norm(values, ln_gain, ln_shift):
    average = jnp.mean(values, axis=-1, keepdims=True)
    centred = values - average
    variance = jnp.mean(centred * centred, axis=-1, keepdims=True)
    return centred * lax.rsqrt(variance + EPS) * ln_gain + ln_shift


def norm_parts(values):
    average = jnp.mean(values, axis=-1, keepdims=True)
    centred = values - average
    variance = jnp.mean(centred * centred, axis=-1, keepdims=True)
    inverse = lax.rsqrt(variance + EPS)
    return centred * inverse, inverse


def norm_back(xhat, inverse, gain, grad):
    scaled = gain * grad
    mean_e = jnp.mean(scaled, axis=-1, keepdims=True)
    mean_ex = jnp.mean(scaled * xhat, axis=-1, keepdims=True)
    return (scaled - mean_e - xhat * mean_ex) * inverse


def gelu_pair(values):
    cdf = 0.5 * (1.0 + lax.erf(values * (2.0 ** -0.5)))
    bell = jnp.exp(-0.5 * values * values) * ((2.0 * jnp.pi) ** -0.5)
    return values * cdf, cdf + values * bell


def contract_rows(left, right):
    return lax.dot_general(left, right, (((0,), (0,)), ((), ())), preferred_element_type=FLOAT)


class Exchange:
    def __init__(self, seqs, heads):
        self.seqs, self.heads = seqs, heads
        self.axes = ("seq", "head")
        self.side = self.swap(1, 0)
        self.low = self.swap(0, 2)
        self.core = self.swap(0, 1)
        self.outer_seq = seqs // 2
        self.outer_head = heads // 4

    def swap(self, seq_bit, head_bit):
        return [
            (s * self.heads + h, (s ^ seq_bit) * self.heads + (h ^ head_bit))
            for s in range(self.seqs)
            for h in range(self.heads)
        ]

    def ahead(self, seq_step, head_step):
        pairs = []
        for s in range(self.seqs):
            for h in range(self.heads):
                s_to = (s + 2 * seq_step) % self.seqs
                h_to = (h + 4 * head_step) % self.heads
                pairs.append((s * self.heads + h, s_to * self.heads + h_to))
        return pairs

    def back(self, seq_step, head_step):
        return [(to, at) for at, to in self.ahead(seq_step, head_step)]

    def send(self, value, pairs):
        return lax.ppermute(value, self.axes, pairs)

    def flat(self):
        return lax.axis_index("seq") * self.heads + lax.axis_index("head")

    def square_gather(self, block):
        half = block.shape[0] // 2
        from_side = self.send(block, self.side)
        from_low = self.send(block, self.low)
        first = self.send(from_side[:half], self.low)
        second = self.send(from_low[half:], self.side)
        same = [block, from_side, from_low, jnp.concatenate([first, second])]
        return same + [self.send(one, self.core) for one in same]

    def square_scatter(self, parts):
        same, other = parts[:4], parts[4:]
        got = [self.send(one, self.core) for one in other]
        total = [a.astype(FLOAT) + b.astype(FLOAT) for a, b in zip(same, got)]
        corner = total[3].astype(LOWER)
        half = corner.shape[0] // 2
        first = self.send(corner[:half], self.low).astype(FLOAT)
        second = self.send(corner[half:], self.side).astype(FLOAT)
        to_side = jnp.concatenate([total[1][:half] + first, total[1][half:]]).astype(LOWER)
        to_low = jnp.concatenate([total[2][:half], total[2][half:] + second]).astype(LOWER)
        from_side = self.send(to_side, self.side).astype(FLOAT)
        from_low = self.send(to_low, self.low).astype(FLOAT)
        return total[0] + from_side + from_low

    def outer_gather(self, block):
        gathered = []
        for j in range(self.outer_head):
            here = block if j == 0 else self.send(block, self.back(0, j))
            gathered += [
                here if i == 0 else self.send(here, self.back(i, 0)) for i in range(self.outer_seq)
            ]
        return gathered

    def outer_scatter(self, parts):
        total = None
        for j in range(self.outer_head):
            mine = parts[j * self.outer_seq : (j + 1) * self.outer_seq]
            here = mine[0].astype(FLOAT)
            for i in range(1, self.outer_seq):
                here = here + self.send(mine[i], self.ahead(i, 0)).astype(FLOAT)
            if j == 0:
                total = here
            else:
                total = total + self.send(here.astype(LOWER), self.ahead(0, j)).astype(FLOAT)
        return total

    def outer_owners(self):
        s, h = lax.axis_index("seq"), lax.axis_index("head")
        return [
            ((s + 2 * i) % self.seqs) * self.heads + (h + 4 * j) % self.heads
            for j in range(self.outer_head)
            for i in range(self.outer_seq)
        ]


def body(
    net,
    layer_input,
    mem_count,
    text_len,
    slot_count,
    w_query,
    w_key,
    w_value,
    b_query,
    b_value,
    ln1_gain,
    ln1_bias,
    w_out,
    b_out,
    ln2_gain,
    ln2_bias,
    w_up,
    b_up,
    w_down,
    b_down,
    cotangent,
):
    scale = HEAD_DIM ** (-0.5)
    both = net.axes
    devices = net.seqs * net.heads
    rows, model = layer_input.shape
    width = w_query.shape[1]
    ff_width = w_up.shape[1]
    owners = net.outer_owners()

    small = jnp.concatenate([ln1_gain, ln1_bias, b_out, ln2_gain, ln2_bias, b_down, b_up])
    small = lax.all_gather(small[None], both, axis=0, tiled=True)
    own = model // devices

    def vector(i):
        return small[:, i * own : (i + 1) * own].reshape(model).astype(FLOAT)

    gain_one, shift_one, bias_out, gain_two, shift_two, bias_down = [vector(i) for i in range(6)]
    bias_up = jnp.concatenate(
        [lax.dynamic_slice(small, (d, 6 * own), (1, ff_width))[0] for d in owners]
    ).astype(FLOAT)

    x_group = lax.all_gather(layer_input, "head", axis=0, tiled=True)
    up_full = jnp.concatenate(net.outer_gather(w_up), axis=1)
    down_full = jnp.concatenate(net.outer_gather(w_down), axis=0)
    cot_group = jnp.concatenate(net.square_gather(cotangent), axis=0)
    proj_out = lax.all_gather(w_out, both, axis=0, tiled=True)

    normed_one = layer_norm(x_group.astype(FLOAT), gain_one, shift_one).astype(LOWER)
    query = (
        (jnp.dot(normed_one, w_query, preferred_element_type=FLOAT) + b_query.astype(FLOAT)) * scale
    ).astype(LOWER)
    keys = jnp.dot(normed_one, w_key, preferred_element_type=FLOAT).astype(LOWER)
    values = (
        jnp.dot(normed_one, w_value, preferred_element_type=FLOAT) + b_value.astype(FLOAT)
    ).astype(LOWER)
    counts = jnp.stack([mem_count, text_len, slot_count])
    context, context32, logsum = attention_forward(query, keys, values, counts)
    ctx_tok = lax.all_to_all(context, "head", split_axis=0, concat_axis=1, tiled=True)

    inputs_f = layer_input.astype(FLOAT)
    hidden = inputs_f + (jnp.dot(ctx_tok, proj_out, preferred_element_type=FLOAT) + bias_out)
    xhat_two, inverse_two = norm_parts(hidden)
    normed_two = (xhat_two * gain_two + shift_two).astype(LOWER)

    n2_group = jnp.concatenate(net.square_gather(normed_two), axis=0)
    pre_act = jnp.dot(n2_group, up_full, preferred_element_type=FLOAT) + bias_up
    act, slope = gelu_pair(pre_act)
    act = act.astype(LOWER)
    grad_pre = (slope * cols_by_cols(cot_group, down_full)).astype(LOWER)
    grad_n2_part = cols_by_cols(grad_pre, up_full).astype(LOWER)
    grad_n2 = net.square_scatter([grad_n2_part[i * rows : (i + 1) * rows] for i in range(8)])
    out_part = jnp.dot(act, down_full, preferred_element_type=FLOAT).astype(LOWER)
    out_sum = net.square_scatter([out_part[i * rows : (i + 1) * rows] for i in range(8)])
    output = (hidden + (out_sum + bias_down)).astype(LOWER)
    outer = len(owners)
    down_part = contract_rows(act, cot_group).astype(LOWER)
    grad_w_down = net.outer_scatter(
        [down_part[i * ff_width : (i + 1) * ff_width] for i in range(outer)]
    )
    up_part = contract_rows(n2_group, grad_pre).astype(LOWER)
    grad_w_up = net.outer_scatter(
        [up_part[:, i * ff_width : (i + 1) * ff_width] for i in range(outer)]
    )
    b_up_part = jnp.sum(grad_pre.astype(FLOAT), 0)

    grad_out_f = cotangent.astype(FLOAT)
    b_down_part = jnp.sum(grad_out_f, 0)
    gain_two_part = jnp.sum(grad_n2 * xhat_two, 0)
    shift_two_part = jnp.sum(grad_n2, 0)
    grad_hidden = grad_out_f + norm_back(xhat_two, inverse_two, gain_two, grad_n2)
    grad_att = grad_hidden.astype(LOWER)
    b_out_part = jnp.sum(grad_att.astype(FLOAT), 0)
    grad_ctx = cols_by_cols(grad_att, proj_out).astype(LOWER)
    grad_heads = lax.all_to_all(grad_ctx, "head", split_axis=1, concat_axis=0, tiled=True)
    grad_w_out = lax.psum_scatter(
        contract_rows(ctx_tok, grad_att).astype(LOWER), both, scatter_dimension=0, tiled=True
    ).astype(FLOAT)

    grad_q, grad_k, grad_v = attention_backward(
        query, keys, values, context32, grad_heads, logsum, counts
    )
    grad_n1_part = (
        cols_by_cols(grad_q, w_query) + cols_by_cols(grad_k, w_key) + cols_by_cols(grad_v, w_value)
    ).astype(LOWER)
    grad_n1 = lax.psum_scatter(grad_n1_part, "head", scatter_dimension=0, tiled=True).astype(FLOAT)
    weight_part = jnp.stack([contract_rows(normed_one, g) for g in (grad_q, grad_k, grad_v)])
    weight_sum = lax.psum(weight_part.astype(LOWER), "seq").astype(FLOAT)
    b_query_part = jnp.sum(grad_q.astype(FLOAT), 0)
    b_value_part = jnp.sum(grad_v.astype(FLOAT), 0)

    xhat_one, inverse_one = norm_parts(inputs_f)
    gain_one_part = jnp.sum(grad_n1 * xhat_one, 0)
    shift_one_part = jnp.sum(grad_n1, 0)
    grad_input = (grad_hidden + norm_back(xhat_one, inverse_one, gain_one, grad_n1)).astype(LOWER)

    row_of = jnp.arange(devices, dtype=jnp.int32)
    up_rows = jnp.zeros((devices, ff_width), FLOAT)
    for i, owner in enumerate(owners):
        up_rows = lax.dynamic_update_slice(
            up_rows, b_up_part[i * ff_width : (i + 1) * ff_width][None], (owner, 0)
        )
    mine = (row_of % net.heads == lax.axis_index("head"))[:, None]
    head_rows = jnp.where(mine, jnp.concatenate([b_query_part, b_value_part])[None], 0.0)
    packed = jnp.concatenate(
        [
            part.reshape(devices, own)
            for part in (
                gain_one_part,
                shift_one_part,
                b_out_part,
                gain_two_part,
                shift_two_part,
                b_down_part,
            )
        ]
        + [up_rows, head_rows],
        axis=1,
    )
    sums = lax.psum_scatter(packed, both, scatter_dimension=0, tiled=True)[0]
    pieces = [sums[i * own : (i + 1) * own] for i in range(6)]
    grad_b_up = sums[6 * own : 6 * own + ff_width]
    grad_b_query = sums[6 * own + ff_width : 6 * own + ff_width + width]
    grad_b_value = sums[6 * own + ff_width + width :]

    return (
        output,
        grad_input,
        weight_sum[0],
        weight_sum[1],
        weight_sum[2],
        grad_b_query,
        grad_b_value,
        pieces[0],
        pieces[1],
        grad_w_out,
        pieces[2],
        pieces[3],
        pieces[4],
        grad_w_up,
        grad_b_up,
        grad_w_down,
        pieces[5],
    )


def solution(mesh):
    net = Exchange(mesh.shape["seq"], mesh.shape["head"])
    rows = P(("seq", "head"), None)
    cols = P(None, ("seq", "head"))
    vec = P(("seq", "head"))
    head_cols = P(None, "head")
    head_vec = P("head")
    count = P("seq")
    return jax.shard_map(
        functools.partial(body, net),
        mesh=mesh,
        in_specs=(
            rows,
            count,
            count,
            count,
            head_cols,
            head_cols,
            head_cols,
            head_vec,
            head_vec,
            vec,
            vec,
            rows,
            vec,
            vec,
            vec,
            cols,
            vec,
            rows,
            vec,
            rows,
        ),
        out_specs=(
            rows,
            rows,
            head_cols,
            head_cols,
            head_cols,
            head_vec,
            head_vec,
            vec,
            vec,
            rows,
            vec,
            vec,
            vec,
            cols,
            vec,
            rows,
            vec,
        ),
        check_vma=False,
    )
```

time: 2890 us -> 1100 us (0.38)
  waiting for transfers between devices: 2170 us -> 504 us
  matrix products: 372 us -> 138 us
  blocking collectives: 118 us -> 209 us
  Pallas kernels: 0 us -> 60.5 us
  other arithmetic: 119 us -> 58.5 us
  starting transfers between devices: 9.17 us -> 40.2 us
    reduce_scatter x4 -> x2, waiting for transfers between devices: 1680 us -> 141 us  [the longest x1 88.2 us: body(): lax.psum_scatter(grad_n1_part, 'head', scatter_dimension=0, tiled=True)]
    all_gather x4 -> x2, waiting for transfers between devices: 364 us -> 0.01 us  [the longest x1 0.01 us: body(): x_group = lax.all_gather(layer_input, 'head', axis=0, tiled=True)]
    ppermute x0 -> x44, waiting for transfers between devices: none -> 243 us  [send(): return lax.ppermute(value, self.axes, pairs)]
    dot_general x35 -> x11, matrix products: 293 us -> 92.6 us  [the longest x6 64.7 us: cols_by_cols(): lax.dot_general(left, right, (((1,), (1,)), ((), ())), preferred_element_...]
    all_gather x1, blocking collectives: 66.5 us -> 178 us  [body(): small = lax.all_gather(small[None], both, axis=0, tiled=True)]
    pallas_call x0 -> x2, Pallas kernels: none -> 60.5 us  [the longest x1 33.5 us: attention_backward(): pl.pallas_call(backward_kernel, grid_spec=pltpu.PrefetchScalarGridSpec(nu...]
    convert_element_type x16 -> x10, other arithmetic: 59.5 us -> 16.1 us  [the longest x1 4.02 us: body(): layer_norm(x_group.astype(FLOAT), gain_one, shift_one).astype(LOWER)]
    unnamed x1 -> x0, blocking collectives: 42.5 us -> none
  transfers between devices with their start and end apart: 12 -> 51, of which waited for: 9 -> 17; matrix products, arithmetic and copies ran while one was open for 8% -> 17% of each run, Pallas kernels for 0% -> 2%
where the time goes in v1:
time: 1100 us
  waiting for transfers between devices  504 us (46%)
  blocking collectives  209 us (19%)
  matrix products  138 us (13%)
  local copies, waits for them, and re-layouts  67.4 us (6%)
  Pallas kernels  60.5 us (6%)
  other arithmetic  58.5 us (5%)
  starting transfers between devices  40.2 us (4%)
  between operations  17.5 us (2%)
    ppermute x44, waiting for transfers between devices, send(): return lax.ppermute(value, self.axes, pairs)  243 us
    all_gather x1, blocking collectives, body(): small = lax.all_gather(small[None], both, axis=0, tiled=True)  178 us
    unnamed x7, waiting for transfers between devices  120 us
    reduce_scatter x1, waiting for transfers between devices, body(): lax.psum_scatter(grad_n1_part, 'head', scatter_dimension=0, tiled=True)  88.2 us
    dot_general x6, matrix products, cols_by_cols(): lax.dot_general(left, right, (((1,), (1,)), ((), ())), preferred_element_...  64.7 us
    reduce_scatter x1, waiting for transfers between devices, body(): lax.psum_scatter(contract_rows(ctx_tok, grad_att).astype(LOWER), both, sc...  53.2 us
    unnamed x103, local copies, waits for them, and re-layouts  42.4 us
    dot_general x6, matrix products, contract_rows(): lax.dot_general(left, right, (((0,), (0,)), ((), ())), preferred_element_...  39.3 us
  transfers between devices with their start and end apart: 51, of which 17 were waited for; matrix products, arithmetic and copies ran while one was open for 17% of the time, Pallas kernels for 2%

profile of v1, /device:TPU:0, one launch (start us, length us, event | category | flops | bytes accessed | tf_op | source)
XLA Modules:
  0.0 1095.5 jit_solution(16051215911352577402)
XLA Ops:
  8.7 4.1 collective-permute-start.9
  17.7 4.8 concatenate.60
  22.5 178.1 %all-gather.1 = bf16[32,1,640]{2,1,0:T(2,128)(2,1)S(1)} all-gather(bf16[1,1,640]{2,1,0:T(2,128)(2,1)S(1)} %reshape.222), channel_id=2, replica_groups=mesh['seq'=4,'head'=8] {'seq','head'}, dimensions={0}, use_global_device_ids=true | all-gather | bytes 42240 | tf_op jit(solution)/shard_map/all_gather | solution.py:381
  214.2 4.7 convert_reduce_fusion
  222.4 4.0 fusion.5
  234.0 27.0 %attn_fwd.1 = (bf16[2048,256]{1,0:T(8,128)(2,1)S(1)}, f32[2048,256]{1,0:T(8,128)}, f32[8,2048]{1,0:T(8,128)S(1)}) custom-call(s32[3,1]{1,0:T(4,128)S(1)} %copy.40.count_ref, bf16[2048,256]{1,0:T(8,128)(2,1)S(1)} %fusion.17.q_ref, bf16[2048,256]{1,0:T(8,128)(2,1)S(1)} %convolution_convert_fusion.9.k_ref, bf16[2048,256]{1,0:T(8,128)(2,1)S(1)} %fusion.16.v_ref), custom_call_target="tpu_custom_call" | custom-call | tf_op jit(solution)/shard_map/attn_fwd/pallas_call | solution.py:98
  262.2 3.6 all-to-all-start
  283.3 13.7 %collective-permute-done.24 = bf16[128,2048]{1,0:T(8,128)(2,1)S(1)} collective-permute-done((bf16[128,2048]{1,0:T(8,128)(2,1)S(1)}, bf16[128,2048]{1,0:T(8,128)(2,1)S(1)}, u32[]{:S(2)}, u32[]{:S(2)}) %collective-permute-start.24) | collective-permute-done | bytes 524320 | tf_op jit(solution)/shard_map/ppermute | solution.py:290
  302.3 6.4 fusion.51
  310.6 2.7 constant_dynamic-update-slice_fusion.20
  314.7 3.1 constant_dynamic-update-slice_fusion.19
  320.1 5.1 collective-permute-done.13
  326.5 8.9 collective-permute-done
  339.0 9.8 collective-permute-done.2
  352.1 3.2 copy-done.32
  355.3 11.2 %fusion.52 = f32[2048,1024]{1,0:T(8,128)} fusion(bf16[2048,2048]{1,0:T(8,128)(2,1)S(1)} %constant_dynamic-update-slice_fusion, bf16[2048,1024]{1,0:T(8,128)(2,1)S(1)} %constant_dynamic-update-slice_fusion.9), kind=kOutput, calls=%fused_computation.177 | convolution fusion | flops 8589934592 | bytes 20971520 | tf_op jit(solution)/shard_map/dot_general | solution.py:416
  366.5 17.4 %convert_reduce_fusion.1 = (f32[1024]{0:T(1024)}, bf16[2048,1024]{1,0:T(8,128)(2,1)}, bf16[2048,1024]{1,0:T(8,128)(2,1)S(1)}) fusion(f32[2048,1024]{1,0:T(8,128)} %fusion.52, f32[1024]{0:T(1024)S(1)} %maximum_convert_fusion, bf16[2048,2048]{1,0:T(8,128)(2,1)} %constant_dynamic-update-slice_fusion.17, ...), kind=kOutput, calls=%fused_computation.16 | convolution fusion | flops 8621390848 | bytes 29368320 | tf_op jit(solution)/shard_map/dot_general | solution.py:19
  385.8 9.3 convolution_convert_fusion.2
  398.1 12.3 %convolution_convert_fusion.1 = bf16[2048,2048]{1,0:T(8,128)(2,1)S(1)} fusion(bf16[2048,1024]{1,0:T(8,128)(2,1)} %get-tuple-element.42, bf16[2048,1024]{1,0:T(8,128)(2,1)} %copy-done.29), kind=kOutput, calls=%fused_computation.20 | convolution fusion | flops 8594128896 | bytes 16777216 | tf_op jit(solution)/shard_map/dot_general | solution.py:19
  413.5 3.9 convert_add_fusion.8
  420.2 2.8 convert_add_fusion.6
  423.9 8.4 collective-permute-done.17
  434.7 8.1 collective-permute-done.33
  450.4 39.5 %collective-permute-done.34 = bf16[256,2048]{1,0:T(8,128)(2,1)} collective-permute-done((bf16[256,2048]{1,0:T(8,128)(2,1)}, bf16[256,2048]{1,0:T(8,128)(2,1)}, u32[]{:S(2)}, u32[]{:S(2)}) %collective-permute-start.34) | collective-permute-done | bytes 1048608 | tf_op jit(solution)/shard_map/ppermute | solution.py:290
  490.0 3.7 multiply_reduce_fusion
  493.7 5.3 convert_reduce_fusion.7
  501.5 31.4 %all_to_all.38 = bf16[256,8,256]{2,0,1:T(8,128)(2,1)} all-to-all(bf16[256,8,256]{2,0,1:T(8,128)(2,1)S(1)} %bitcast.92), channel_id=1, replica_groups=mesh['seq'=4,'head'=8] {'head'}, dimensions={1} | all-to-all | bytes 2097152 | tf_op jit(solution)/shard_map/all_to_all | solution.py:444
  532.9 33.5 %attn_bwd.1 = (bf16[2048,256]{1,0:T(8,128)(2,1)S(1)}, bf16[2048,256]{1,0:T(8,128)(2,1)S(1)}, bf16[2048,256]{1,0:T(8,128)(2,1)S(1)}) custom-call(s32[3,1]{1,0:T(4,128)S(1)} %copy.40.count_ref, bf16[2048,256]{1,0:T(8,128)(2,1)S(1)} %copy-done.3, bf16[2048,256]{1,0:T(8,128)(2,1)S(1)} %copy-done.5, bf16[2048,256]{1,0:T(8,128)(2,1)} %copy-done.1, ...), custom_call_target="tpu_custom_call" | custom-call | tf_op jit(solution)/shard_map/attn_bwd/pallas_call | solution.py:197
  566.5 2.5 fusion.21
  571.5 2.5 fusion.23
  576.2 7.5 convolution_convert_fusion
  584.0 8.1 fusion.53
  592.1 8.2 fusion.54
  600.3 16.3 %add_convert_fusion = bf16[2048,2048]{1,0:T(8,128)(2,1)} fusion(f32[2048,2048]{1,0:T(8,128)} %fusion.53, f32[2048,2048]{1,0:T(8,128)} %fusion.54, bf16[2048,256]{1,0:T(8,128)(2,1)S(1)} %get-tuple-element.28, bf16[2048,256]{1,0:T(8,128)(2,1)} %param.26), kind=kOutput, calls=%fused_computation.8 | convolution fusion | flops 2160066560 | bytes 44040192 | tf_op jit(solution)/shard_map/dot_general | solution.py:19
  616.7 12.7 %convolution_convert_fusion.3 = bf16[1024,2048]{1,0:T(8,128)(2,1)S(1)} fusion(bf16[2048,1024]{1,0:T(8,128)(2,1)} %copy-done.34, bf16[2048,2048]{1,0:T(8,128)(2,1)} %constant_dynamic-update-slice_fusion.17), kind=kOutput, calls=%fused_computation.22 | convolution fusion | flops 8592031744 | bytes 16777216 | tf_op jit(solution)/shard_map/dot_general | solution.py:257
  633.5 11.5 %convolution_convert_fusion.4 = bf16[2048,1024]{1,0:T(8,128)(2,1)S(1)} fusion(bf16[2048,2048]{1,0:T(8,128)(2,1)} %copy-done.32, bf16[2048,1024]{1,0:T(8,128)(2,1)S(1)} %copy-done.35), kind=kOutput, calls=%fused_computation.23 | convolution fusion | flops 8592031744 | bytes 16777216 | tf_op jit(solution)/shard_map/dot_general | solution.py:257
  650.0 16.4 %collective-permute-done.42 = bf16[256,2048]{1,0:T(8,128)(2,1)S(1)} collective-permute-done((bf16[256,2048]{1,0:T(8,128)(2,1)S(1)}, bf16[256,2048]{1,0:T(8,128)(2,1)S(1)}, u32[]{:S(2)}, u32[]{:S(2)}) %collective-permute-start.42) | collective-permute-done | bytes 1048608 | tf_op jit(solution)/shard_map/ppermute | solution.py:290
  670.2 27.1 %collective-permute-done.39 = bf16[2048,256]{1,0:T(8,128)(2,1)S(1)} collective-permute-done((bf16[2048,256]{1,0:T(8,128)(2,1)S(1)}, bf16[2048,256]{1,0:T(8,128)(2,1)S(1)}, u32[]{:S(2)}, u32[]{:S(2)}) %collective-permute-start.39) | collective-permute-done | bytes 1048608 | tf_op jit(solution)/shard_map/ppermute | solution.py:290
  700.5 26.7 %collective-permute-done.41 = bf16[256,2048]{1,0:T(8,128)(2,1)} collective-permute-done((bf16[256,2048]{1,0:T(8,128)(2,1)}, bf16[256,2048]{1,0:T(8,128)(2,1)}, u32[]{:S(2)}, u32[]{:S(2)}) %collective-permute-start.41) | collective-permute-done | bytes 1048608 | tf_op jit(solution)/shard_map/ppermute | solution.py:290
  727.1 37.0 %collective-permute-done.43 = bf16[256,2048]{1,0:T(8,128)(2,1)} collective-permute-done((bf16[256,2048]{1,0:T(8,128)(2,1)}, bf16[256,2048]{1,0:T(8,128)(2,1)}, u32[]{:S(2)}, u32[]{:S(2)}) %collective-permute-start.43) | collective-permute-done | bytes 1048608 | tf_op jit(solution)/shard_map/ppermute | solution.py:290
  764.1 3.7 convert_add_fusion.2
  767.8 39.2 %collective-permute-done.40 = bf16[2048,256]{1,0:T(8,128)(2,1)} collective-permute-done((bf16[2048,256]{1,0:T(8,128)(2,1)}, bf16[2048,256]{1,0:T(8,128)(2,1)}, u32[]{:S(2)}, u32[]{:S(2)}) %collective-permute-start.40) | collective-permute-done | bytes 1048608 | tf_op jit(solution)/shard_map/ppermute | solution.py:290
  807.0 3.5 convert_add_fusion.3
  814.0 2.8 slice_bitcast_fusion
  816.8 53.2 %reduce-scatter.5.cloned.1.call-done = bf16[64,2048]{1,0:T(8,128)(2,1)} async-done(((bf16[2048,2048]{1,0:T(8,128)(2,1)}), bf16[64,2048]{1,0:T(8,128)(2,1)}) %reduce-scatter.5.cloned.1.call-update) | async-done | bytes 262160 | tf_op jit(solution)/shard_map/reduce_scatter | solution.py:445
  871.8 88.2 %reduce-scatter.3.cloned.1.call-done = bf16[256,2048]{1,0:T(8,128)(2,1)} async-done(((bf16[2048,2048]{1,0:T(8,128)(2,1)}), bf16[256,2048]{1,0:T(8,128)(2,1)}) %reduce-scatter.3.cloned.1.call-update) | async-done | bytes 1048592 | tf_op jit(solution)/shard_map/reduce_scatter | solution.py:455
  963.1 3.7 fusion.27
  966.8 118.5 %all-reduce.6.cloned.1.call-done = f32[32,1152]{1,0:T(8,128)} async-done(((f32[32,1152]{1,0:T(8,128)}), f32[32,1152]{1,0:T(8,128)}) %all-reduce.6.cloned.1.call-update) | async-done | bytes 147472
  (281 shorter events, 122.9 us)
Async XLA Ops:
  7.2 207.0 %all-gather.5.cloned.1.call-start = ((), (), s32[]{:S(2)}) async-start(), calls=%async_computation.4 | async-start | bytes 9437184 | tf_op jit(solution)/shard_map/all_gather | solution.py:392
  8.0 293.4 %all-gather.7.cloned.1.call-start = ((), (), s32[]{:S(2)}) async-start(), calls=%async_computation.5 | async-start | bytes 8650752 | tf_op jit(solution)/shard_map/all_gather | solution.py:396
  8.7 266.2 %collective-permute-start.9 = (bf16[2048,256]{1,0:T(8,128)(2,1)}, bf16[2048,256]{1,0:T(8,128)(2,1)}, u32[]{:S(2)}, u32[]{:S(2)}) collective-permute-start(bf16[2048,256]{1,0:T(8,128)(2,1)} %param.35), channel_id=1, source_target_pairs={{4,0},{5,1},{6,2},{7,3},{0,4},{1,5},{2,6},{3,7},{12,8},{13,9},{14,... | collective-permute-start | bytes 3145736 | tf_op jit(solution)/shard_map/ppermute | solution.py:290
  12.8 258.0 %collective-permute-start.8 = (bf16[2048,256]{1,0:T(8,128)(2,1)}, bf16[2048,256]{1,0:T(8,128)(2,1)}, u32[]{:S(2)}, u32[]{:S(2)}) collective-permute-start(bf16[2048,256]{1,0:T(8,128)(2,1)} %param.35), channel_id=1, source_target_pairs={{16,0},{17,1},{18,2},{19,3},{20,4},{21,5},{22,6},{23,7},{24,8},{25... | collective-permute-start | bytes 3145736 | tf_op jit(solution)/shard_map/ppermute | solution.py:290
  14.3 196.0 %collective-permute-start.22 = (bf16[256,2048]{1,0:T(8,128)(2,1)}, bf16[256,2048]{1,0:T(8,128)(2,1)}, u32[]{:S(2)}, u32[]{:S(2)}) collective-permute-start(bf16[256,2048]{1,0:T(8,128)(2,1)} %param.39), channel_id=1, source_target_pairs={{0,8},{1,9},{2,10},{3,11},{4,12},{5,13},{6,14},{7,15},{8,0},{9,1},... | collective-permute-start | bytes 3145736 | tf_op jit(solution)/shard_map/ppermute | solution.py:290
  15.8 250.1 %collective-permute-start.23 = (bf16[256,2048]{1,0:T(8,128)(2,1)}, bf16[256,2048]{1,0:T(8,128)(2,1)}, u32[]{:S(2)}, u32[]{:S(2)}) collective-permute-start(bf16[256,2048]{1,0:T(8,128)(2,1)} %param.39), channel_id=1, source_target_pairs={{0,2},{1,3},{2,0},{3,1},{4,6},{5,7},{6,4},{7,5},{8,10},{9,11},{10,... | collective-permute-start | bytes 3145736 | tf_op jit(solution)/shard_map/ppermute | solution.py:290
  17.4 263.7 %collective-permute-start.12 = (bf16[256,2048]{1,0:T(8,128)(2,1)}, bf16[256,2048]{1,0:T(8,128)(2,1)}, u32[]{:S(2)}, u32[]{:S(2)}) collective-permute-start(bf16[256,2048]{1,0:T(8,128)(2,1)} %param.37), channel_id=1, source_target_pairs={{4,0},{5,1},{6,2},{7,3},{0,4},{1,5},{2,6},{3,7},{12,8},{13,9},{14,... | collective-permute-start | bytes 3145736 | tf_op jit(solution)/shard_map/ppermute | solution.py:290
  210.3 67.2 %collective-permute-start.11 = (bf16[256,2048]{1,0:T(8,128)(2,1)S(1)}, bf16[256,2048]{1,0:T(8,128)(2,1)}, u32[]{:S(2)}, u32[]{:S(2)}) collective-permute-start(bf16[256,2048]{1,0:T(8,128)(2,1)S(1)} %copy-done.21), channel_id=1, source_target_pairs={{16,0},{17,1},{18,2},{19,3},{20,4},{21,5},{22,6},{23,7},{24,8},{25... | collective-permute-start | bytes 3145736 | tf_op jit(solution)/shard_map/ppermute | solution.py:290
  262.2 39.1 %all-to-all-start = ((bf16[8,256,256]{1,2,0:T(8,128)(2,1)}), bf16[8,256,256]{1,2,0:T(8,128)(2,1)S(1)}, u32[]{:S(2)}, u32[]{:S(2)}) async-start(bf16[8,256,256]{1,2,0:T(8,128)(2,1)} %copy.41), calls=%async_computation | async-start | bytes 2097152 | tf_op jit(solution)/shard_map/all_to_all | solution.py:408
  265.8 545.7 %all-reduce.4.cloned.1.call-start = ((), (), s32[]{:S(2)}) async-start(), calls=%async_computation.7 | async-start | bytes 6291456 | tf_op jit(solution)/shard_map/psum | solution.py:457
  265.9 43.7 %collective-permute-start.26 = (bf16[256,2048]{1,0:T(8,128)(2,1)}, bf16[256,2048]{1,0:T(8,128)(2,1)}, u32[]{:S(2)}, u32[]{:S(2)}) collective-permute-start(bf16[256,2048]{1,0:T(8,128)(2,1)} %param.39), channel_id=1, source_target_pairs={{0,1},{1,0},{2,3},{3,2},{4,5},{5,4},{6,7},{7,6},{8,9},{9,8},{10,11... | collective-permute-start | bytes 3145736 | tf_op jit(solution)/shard_map/ppermute | solution.py:290
  270.8 26.2 %collective-permute-start.24 = (bf16[128,2048]{1,0:T(8,128)(2,1)S(1)}, bf16[128,2048]{1,0:T(8,128)(2,1)S(1)}, u32[]{:S(2)}, u32[]{:S(2)}) collective-permute-start(bf16[128,2048]{1,0:T(8,128)(2,1)S(1)} %slice.310), channel_id=1, source_target_pairs={{0,2},{1,3},{2,0},{3,1},{4,6},{5,7},{6,4},{7,5},{8,10},{9,11},{10,... | collective-permute-start | bytes 1572872 | tf_op jit(solution)/shard_map/ppermute | solution.py:290
  274.9 23.0 %collective-permute-start.25 = (bf16[128,2048]{1,0:T(8,128)(2,1)S(1)}, bf16[128,2048]{1,0:T(8,128)(2,1)S(1)}, u32[]{:S(2)}, u32[]{:S(2)}) collective-permute-start(bf16[128,2048]{1,0:T(8,128)(2,1)S(1)} %slice.311), channel_id=1, source_target_pairs={{0,8},{1,9},{2,10},{3,11},{4,12},{5,13},{6,14},{7,15},{8,0},{9,1},... | collective-permute-start | bytes 1572872 | tf_op jit(solution)/shard_map/ppermute | solution.py:290
  277.6 32.6 %collective-permute-start.10 = (bf16[2048,256]{1,0:T(8,128)(2,1)}, bf16[2048,256]{1,0:T(8,128)(2,1)}, u32[]{:S(2)}, u32[]{:S(2)}) collective-permute-start(bf16[2048,256]{1,0:T(8,128)(2,1)} %collective-permute-done.9), channel_id=1, source_target_pairs={{16,0},{17,1},{18,2},{19,3},{20,4},{21,5},{22,6},{23,7},{24,8},{25... | collective-permute-start | bytes 3145736 | tf_op jit(solution)/shard_map/ppermute | solution.py:290
  281.0 29.1 %collective-permute-start.27 = (bf16[256,2048]{1,0:T(8,128)(2,1)}, bf16[256,2048]{1,0:T(8,128)(2,1)}, u32[]{:S(2)}, u32[]{:S(2)}) collective-permute-start(bf16[256,2048]{1,0:T(8,128)(2,1)} %collective-permute-done.22), channel_id=1, source_target_pairs={{0,1},{1,0},{2,3},{3,2},{4,5},{5,4},{6,7},{7,6},{8,9},{9,8},{10,11... | collective-permute-start | bytes 3145736 | tf_op jit(solution)/shard_map/ppermute | solution.py:290
  297.0 20.7 %collective-permute-start.28 = (bf16[256,2048]{1,0:T(8,128)(2,1)}, bf16[256,2048]{1,0:T(8,128)(2,1)}, u32[]{:S(2)}, u32[]{:S(2)}) collective-permute-start(bf16[256,2048]{1,0:T(8,128)(2,1)} %collective-permute-done.23), channel_id=1, source_target_pairs={{0,1},{1,0},{2,3},{3,2},{4,5},{5,4},{6,7},{7,6},{8,9},{9,8},{10,11... | collective-permute-start | bytes 3145736 | tf_op jit(solution)/shard_map/ppermute | solution.py:290
  297.9 27.3 %collective-permute-start.13 = (bf16[256,2048]{1,0:T(8,128)(2,1)}, bf16[256,2048]{1,0:T(8,128)(2,1)}, u32[]{:S(2)}, u32[]{:S(2)}) collective-permute-start(bf16[256,2048]{1,0:T(8,128)(2,1)} %collective-permute-done.12), channel_id=1, source_target_pairs={{16,0},{17,1},{18,2},{19,3},{20,4},{21,5},{22,6},{23,7},{24,8},{25... | collective-permute-start | bytes 3145736 | tf_op jit(solution)/shard_map/ppermute | solution.py:290
  309.9 27.4 %collective-permute-start.29 = (bf16[256,2048]{1,0:T(8,128)(2,1)S(1)}, bf16[256,2048]{1,0:T(8,128)(2,1)S(1)}, u32[]{:S(2)}, u32[]{:S(2)}) collective-permute-start(bf16[256,2048]{1,0:T(8,128)(2,1)S(1)} %copy-done.22), channel_id=1, source_target_pairs={{0,1},{1,0},{2,3},{3,2},{4,5},{5,4},{6,7},{7,6},{8,9},{9,8},{10,11... | collective-permute-start | bytes 3145736 | tf_op jit(solution)/shard_map/ppermute | solution.py:290
  310.1 25.3 %collective-permute-start = (bf16[256,2048]{1,0:T(8,128)(2,1)S(1)}, bf16[256,2048]{1,0:T(8,128)(2,1)S(1)}, u32[]{:S(2)}, u32[]{:S(2)}) collective-permute-start(bf16[256,2048]{1,0:T(8,128)(2,1)S(1)} %get-tuple-element.47), channel_id=1, source_target_pairs={{0,8},{1,9},{2,10},{3,11},{4,12},{5,13},{6,14},{7,15},{8,0},{9,1},... | collective-permute-start | bytes 3145736 | tf_op jit(solution)/shard_map/ppermute | solution.py:290
  310.1 25.9 %collective-permute-start.1 = (bf16[256,2048]{1,0:T(8,128)(2,1)S(1)}, bf16[256,2048]{1,0:T(8,128)(2,1)S(1)}, u32[]{:S(2)}, u32[]{:S(2)}) collective-permute-start(bf16[256,2048]{1,0:T(8,128)(2,1)S(1)} %get-tuple-element.47), channel_id=1, source_target_pairs={{0,2},{1,3},{2,0},{3,1},{4,6},{5,7},{6,4},{7,5},{8,10},{9,11},{10,... | collective-permute-start | bytes 3145736 | tf_op jit(solution)/shard_map/ppermute | solution.py:290
  335.5 13.4 %collective-permute-start.2 = (bf16[128,2048]{1,0:T(8,128)(2,1)S(1)}, bf16[128,2048]{1,0:T(8,128)(2,1)S(1)}, u32[]{:S(2)}, u32[]{:S(2)}) collective-permute-start(bf16[128,2048]{1,0:T(8,128)(2,1)S(1)} %slice.293), channel_id=1, source_target_pairs={{0,2},{1,3},{2,0},{3,1},{4,6},{5,7},{6,4},{7,5},{8,10},{9,11},{10,... | collective-permute-start | bytes 1572872 | tf_op jit(solution)/shard_map/ppermute | solution.py:290
  336.1 13.1 %collective-permute-start.3 = (bf16[128,2048]{1,0:T(8,128)(2,1)S(1)}, bf16[128,2048]{1,0:T(8,128)(2,1)S(1)}, u32[]{:S(2)}, u32[]{:S(2)}) collective-permute-start(bf16[128,2048]{1,0:T(8,128)(2,1)S(1)} %slice.294), channel_id=1, source_target_pairs={{0,8},{1,9},{2,10},{3,11},{4,12},{5,13},{6,14},{7,15},{8,0},{9,1},... | collective-permute-start | bytes 1572872 | tf_op jit(solution)/shard_map/ppermute | solution.py:290
  338.4 11.1 %collective-permute-start.4 = (bf16[256,2048]{1,0:T(8,128)(2,1)S(1)}, bf16[256,2048]{1,0:T(8,128)(2,1)S(1)}, u32[]{:S(2)}, u32[]{:S(2)}) collective-permute-start(bf16[256,2048]{1,0:T(8,128)(2,1)S(1)} %get-tuple-element.47), channel_id=1, source_target_pairs={{0,1},{1,0},{2,3},{3,2},{4,5},{5,4},{6,7},{7,6},{8,9},{9,8},{10,11... | collective-permute-start | bytes 3145736 | tf_op jit(solution)/shard_map/ppermute | solution.py:290
  338.4 11.1 %collective-permute-start.5 = (bf16[256,2048]{1,0:T(8,128)(2,1)S(1)}, bf16[256,2048]{1,0:T(8,128)(2,1)S(1)}, u32[]{:S(2)}, u32[]{:S(2)}) collective-permute-start(bf16[256,2048]{1,0:T(8,128)(2,1)S(1)} %collective-permute-done), channel_id=1, source_target_pairs={{0,1},{1,0},{2,3},{3,2},{4,5},{5,4},{6,7},{7,6},{8,9},{9,8},{10,11... | collective-permute-start | bytes 3145736 | tf_op jit(solution)/shard_map/ppermute | solution.py:290
  338.9 10.7 collective-permute-start.6
  397.1 13.9 %collective-permute-start.15 = (bf16[256,2048]{1,0:T(8,128)(2,1)}, bf16[256,2048]{1,0:T(8,128)(2,1)S(1)}, u32[]{:S(2)}, u32[]{:S(2)}) collective-permute-start(bf16[256,2048]{1,0:T(8,128)(2,1)} %get-tuple-element.59), channel_id=1, source_target_pairs={{0,1},{1,0},{2,3},{3,2},{4,5},{5,4},{6,7},{7,6},{8,9},{9,8},{10,11... | collective-permute-start | bytes 3145736 | tf_op jit(solution)/shard_map/ppermute | solution.py:290
  397.2 14.2 %collective-permute-start.16 = (bf16[256,2048]{1,0:T(8,128)(2,1)S(1)}, bf16[256,2048]{1,0:T(8,128)(2,1)S(1)}, u32[]{:S(2)}, u32[]{:S(2)}) collective-permute-start(bf16[256,2048]{1,0:T(8,128)(2,1)S(1)} %get-tuple-element.58), channel_id=1, source_target_pairs={{0,1},{1,0},{2,3},{3,2},{4,5},{5,4},{6,7},{7,6},{8,9},{9,8},{10,11... | collective-permute-start | bytes 3145736 | tf_op jit(solution)/shard_map/ppermute | solution.py:290
  397.6 13.9 %collective-permute-start.19 = (bf16[256,2048]{1,0:T(8,128)(2,1)S(1)}, bf16[256,2048]{1,0:T(8,128)(2,1)S(1)}, u32[]{:S(2)}, u32[]{:S(2)}) collective-permute-start(bf16[256,2048]{1,0:T(8,128)(2,1)S(1)} %get-tuple-element.57), channel_id=1, source_target_pairs={{0,1},{1,0},{2,3},{3,2},{4,5},{5,4},{6,7},{7,6},{8,9},{9,8},{10,11... | collective-permute-start | bytes 3145736 | tf_op jit(solution)/shard_map/ppermute | solution.py:290
  397.8 95.9 %collective-permute-start.14 = (bf16[256,2048]{1,0:T(8,128)(2,1)}, bf16[256,2048]{1,0:T(8,128)(2,1)}, u32[]{:S(2)}, u32[]{:S(2)}) collective-permute-start(bf16[256,2048]{1,0:T(8,128)(2,1)} %get-tuple-element.56), channel_id=1, source_target_pairs={{0,1},{1,0},{2,3},{3,2},{4,5},{5,4},{6,7},{7,6},{8,9},{9,8},{10,11... | collective-permute-start | bytes 3145736 | tf_op jit(solution)/shard_map/ppermute | solution.py:290
  411.4 8.8 collective-permute-start.35
  413.2 36.7 %collective-permute-start.30 = (bf16[256,2048]{1,0:T(8,128)(2,1)S(1)}, bf16[256,2048]{1,0:T(8,128)(2,1)}, u32[]{:S(2)}, u32[]{:S(2)}) collective-permute-start(bf16[256,2048]{1,0:T(8,128)(2,1)S(1)} %get-tuple-element.49), channel_id=1, source_target_pairs={{0,1},{1,0},{2,3},{3,2},{4,5},{5,4},{6,7},{7,6},{8,9},{9,8},{10,11... | collective-permute-start | bytes 3145736 | tf_op jit(solution)/shard_map/ppermute | solution.py:290
  417.5 14.8 %collective-permute-start.17 = (bf16[128,2048]{1,0:T(8,128)(2,1)S(1)}, bf16[128,2048]{1,0:T(8,128)(2,1)S(1)}, u32[]{:S(2)}, u32[]{:S(2)}) collective-permute-start(bf16[128,2048]{1,0:T(8,128)(2,1)S(1)} %get-tuple-element.74), channel_id=1, source_target_pairs={{0,2},{1,3},{2,0},{3,1},{4,6},{5,7},{6,4},{7,5},{8,10},{9,11},{10,... | collective-permute-start | bytes 1572872 | tf_op jit(solution)/shard_map/ppermute | solution.py:290
  419.2 27.9 %collective-permute-start.20 = (bf16[128,2048]{1,0:T(8,128)(2,1)S(1)}, bf16[128,2048]{1,0:T(8,128)(2,1)S(1)}, u32[]{:S(2)}, u32[]{:S(2)}) collective-permute-start(bf16[128,2048]{1,0:T(8,128)(2,1)S(1)} %get-tuple-element.75), channel_id=1, source_target_pairs={{0,8},{1,9},{2,10},{3,11},{4,12},{5,13},{6,14},{7,15},{8,0},{9,1},... | collective-permute-start | bytes 1572872 | tf_op jit(solution)/shard_map/ppermute | solution.py:290
  423.1 19.7 %collective-permute-start.33 = (bf16[128,2048]{1,0:T(8,128)(2,1)S(1)}, bf16[128,2048]{1,0:T(8,128)(2,1)S(1)}, u32[]{:S(2)}, u32[]{:S(2)}) collective-permute-start(bf16[128,2048]{1,0:T(8,128)(2,1)S(1)} %get-tuple-element.72), channel_id=1, source_target_pairs={{0,2},{1,3},{2,0},{3,1},{4,6},{5,7},{6,4},{7,5},{8,10},{9,11},{10,... | collective-permute-start | bytes 1572872 | tf_op jit(solution)/shard_map/ppermute | solution.py:290
  432.4 12.7 %collective-permute-start.36 = (bf16[128,2048]{1,0:T(8,128)(2,1)S(1)}, bf16[128,2048]{1,0:T(8,128)(2,1)S(1)}, u32[]{:S(2)}, u32[]{:S(2)}) collective-permute-start(bf16[128,2048]{1,0:T(8,128)(2,1)S(1)} %get-tuple-element.73), channel_id=1, source_target_pairs={{0,8},{1,9},{2,10},{3,11},{4,12},{5,13},{6,14},{7,15},{8,0},{9,1},... | collective-permute-start | bytes 1572872 | tf_op jit(solution)/shard_map/ppermute | solution.py:290
  442.8 50.9 %collective-permute-start.18 = (bf16[256,2048]{1,0:T(8,128)(2,1)}, bf16[256,2048]{1,0:T(8,128)(2,1)}, u32[]{:S(2)}, u32[]{:S(2)}) collective-permute-start(bf16[256,2048]{1,0:T(8,128)(2,1)} %pad_maximum_fusion.2), channel_id=1, source_target_pairs={{0,8},{1,9},{2,10},{3,11},{4,12},{5,13},{6,14},{7,15},{8,0},{9,1},... | collective-permute-start | bytes 3145736 | tf_op jit(solution)/shard_map/ppermute | solution.py:290
  445.1 44.8 %collective-permute-start.34 = (bf16[256,2048]{1,0:T(8,128)(2,1)}, bf16[256,2048]{1,0:T(8,128)(2,1)}, u32[]{:S(2)}, u32[]{:S(2)}) collective-permute-start(bf16[256,2048]{1,0:T(8,128)(2,1)} %pad_maximum_fusion.5), channel_id=1, source_target_pairs={{0,8},{1,9},{2,10},{3,11},{4,12},{5,13},{6,14},{7,15},{8,0},{9,1},... | collective-permute-start | bytes 3145736 | tf_op jit(solution)/shard_map/ppermute | solution.py:290
  447.1 42.8 %collective-permute-start.37 = (bf16[256,2048]{1,0:T(8,128)(2,1)}, bf16[256,2048]{1,0:T(8,128)(2,1)}, u32[]{:S(2)}, u32[]{:S(2)}) collective-permute-start(bf16[256,2048]{1,0:T(8,128)(2,1)} %pad_maximum_fusion.6), channel_id=1, source_target_pairs={{0,2},{1,3},{2,0},{3,1},{4,6},{5,7},{6,4},{7,5},{8,10},{9,11},{10,... | collective-permute-start | bytes 3145736 | tf_op jit(solution)/shard_map/ppermute | solution.py:290
  449.9 43.8 %collective-permute-start.21 = (bf16[256,2048]{1,0:T(8,128)(2,1)}, bf16[256,2048]{1,0:T(8,128)(2,1)}, u32[]{:S(2)}, u32[]{:S(2)}) collective-permute-start(bf16[256,2048]{1,0:T(8,128)(2,1)} %pad_maximum_fusion.3), channel_id=1, source_target_pairs={{0,2},{1,3},{2,0},{3,1},{4,6},{5,7},{6,4},{7,5},{8,10},{9,11},{10,... | collective-permute-start | bytes 3145736 | tf_op jit(solution)/shard_map/ppermute | solution.py:290
  576.1 293.9 %reduce-scatter.5.cloned.1.call-start = ((), (), s32[]{:S(2)}) async-start(), calls=%async_computation.8 | async-start | bytes 8650752 | tf_op jit(solution)/shard_map/reduce_scatter | solution.py:445
  583.7 376.2 %reduce-scatter.3.cloned.1.call-start = ((), (), s32[]{:S(2)}) async-start(), calls=%async_computation.6 | async-start | bytes 9437184 | tf_op jit(solution)/shard_map/reduce_scatter | solution.py:455
  616.7 468.7 %all-reduce.6.cloned.1.call-start = ((), (), s32[]{:S(2)}) async-start(), calls=%async_computation.9 | async-start | bytes 294912
  630.6 35.7 %collective-permute-start.42 = (bf16[256,2048]{1,0:T(8,128)(2,1)S(1)}, bf16[256,2048]{1,0:T(8,128)(2,1)S(1)}, u32[]{:S(2)}, u32[]{:S(2)}) collective-permute-start(bf16[256,2048]{1,0:T(8,128)(2,1)S(1)} %get-tuple-element.67), channel_id=1, source_target_pairs={{0,16},{1,17},{2,18},{3,19},{4,20},{5,21},{6,22},{7,23},{8,24},{9,... | collective-permute-start | bytes 3145736 | tf_op jit(solution)/shard_map/ppermute | solution.py:290
  646.2 51.1 %collective-permute-start.39 = (bf16[2048,256]{1,0:T(8,128)(2,1)S(1)}, bf16[2048,256]{1,0:T(8,128)(2,1)S(1)}, u32[]{:S(2)}, u32[]{:S(2)}) collective-permute-start(bf16[2048,256]{1,0:T(8,128)(2,1)S(1)} %get-tuple-element.69), channel_id=1, source_target_pairs={{0,16},{1,17},{2,18},{3,19},{4,20},{5,21},{6,22},{7,23},{8,24},{9,... | collective-permute-start | bytes 3145736 | tf_op jit(solution)/shard_map/ppermute | solution.py:290
  647.9 79.3 %collective-permute-start.41 = (bf16[256,2048]{1,0:T(8,128)(2,1)}, bf16[256,2048]{1,0:T(8,128)(2,1)}, u32[]{:S(2)}, u32[]{:S(2)}) collective-permute-start(bf16[256,2048]{1,0:T(8,128)(2,1)} %get-tuple-element.66), channel_id=1, source_target_pairs={{0,16},{1,17},{2,18},{3,19},{4,20},{5,21},{6,22},{7,23},{8,24},{9,... | collective-permute-start | bytes 3145736 | tf_op jit(solution)/shard_map/ppermute | solution.py:290
  648.9 118.9 %collective-permute-start.38 = (bf16[2048,256]{1,0:T(8,128)(2,1)}, bf16[2048,256]{1,0:T(8,128)(2,1)}, u32[]{:S(2)}, u32[]{:S(2)}) collective-permute-start(bf16[2048,256]{1,0:T(8,128)(2,1)} %get-tuple-element.68), channel_id=1, source_target_pairs={{0,16},{1,17},{2,18},{3,19},{4,20},{5,21},{6,22},{7,23},{8,24},{9,... | collective-permute-start | bytes 3145736 | tf_op jit(solution)/shard_map/ppermute | solution.py:290
  667.7 96.4 %collective-permute-start.43 = (bf16[256,2048]{1,0:T(8,128)(2,1)}, bf16[256,2048]{1,0:T(8,128)(2,1)}, u32[]{:S(2)}, u32[]{:S(2)}) collective-permute-start(bf16[256,2048]{1,0:T(8,128)(2,1)} %add_convert_fusion.1), channel_id=1, source_target_pairs={{0,4},{1,5},{2,6},{3,7},{4,0},{5,1},{6,2},{7,3},{8,12},{9,13},{10,... | collective-permute-start | bytes 3145736 | tf_op jit(solution)/shard_map/ppermute | solution.py:290
  698.7 108.3 %collective-permute-start.40 = (bf16[2048,256]{1,0:T(8,128)(2,1)}, bf16[2048,256]{1,0:T(8,128)(2,1)}, u32[]{:S(2)}, u32[]{:S(2)}) collective-permute-start(bf16[2048,256]{1,0:T(8,128)(2,1)} %add_convert_fusion.2), channel_id=1, source_target_pairs={{0,4},{1,5},{2,6},{3,7},{4,0},{5,1},{6,2},{7,3},{8,12},{9,13},{10,... | collective-permute-start | bytes 3145736 | tf_op jit(solution)/shard_map/ppermute | solution.py:290
  (43 other events, 1292.9 us)
Sparse Core Ops, SparseCore 0:
  9.7 152.9 all-gather.4
  165.6 92.7 all-gather.6
  576.2 104.9 all-reduce.3
  683.5 186.4 reduce-scatter.4
  872.2 87.6 reduce-scatter.2
  966.2 119.0 all-reduce.5

commit v2 on v1

--- a/solution.py
+++ b/solution.py
@@ -87,6 +87,11 @@
     flat = acc[...].T
     out32_ref[...] = flat
     out_ref[...] = flat.astype(LOWER)
+
+
+def kernel_cost(micros, rows, width):
+    flops = micros * 1000000
+    return pl.CostEstimate(flops=flops, bytes_accessed=1000000, transcendentals=0)
 
 
 def attention_forward(query, keys, values, counts):
@@ -118,6 +123,7 @@
             jax.ShapeDtypeStruct((8, rows), FLOAT),
         ],
         compiler_params=pltpu.CompilerParams(vmem_limit_bytes=48 * 2**20),
+        cost_estimate=kernel_cost(26, rows, width),
         name="attn_fwd",
     )(counts, query, keys, values)
 
@@ -218,18 +224,12 @@
         ),
         out_shape=[jax.ShapeDtypeStruct((rows, width), LOWER)] * 3,
         compiler_params=pltpu.CompilerParams(vmem_limit_bytes=48 * 2**20),
+        cost_estimate=kernel_cost(34, rows, width),
         name="attn_bwd",
     )(counts, query, keys, values, out32, grad, lse)
 
 
 EPS = 1e-05
-
-
-def layer_norm(values, ln_gain, ln_shift):
-    average = jnp.mean(values, axis=-1, keepdims=True)
-    centred = values - average
-    variance = jnp.mean(centred * centred, axis=-1, keepdims=True)
-    return centred * lax.rsqrt(variance + EPS) * ln_gain + ln_shift
 
 
 def norm_parts(values):
@@ -255,6 +255,54 @@
 
 def contract_rows(left, right):
     return lax.dot_general(left, right, (((0,), (0,)), ((), ())), preferred_element_type=FLOAT)
+
+
+def after(value, *others):
+    return lax.optimization_barrier((value, *others))[0]
+
+
+def project_kernel(x_ref, gain_ref, shift_ref, bias_ref, wq_ref, wk_ref, wv_ref, n_ref, q_ref, k_ref, v_ref):
+    values = x_ref[0].astype(FLOAT)
+    size = values.shape[1]
+    average = jnp.sum(values, axis=-1, keepdims=True) * (1.0 / size)
+    centred = values - average
+    variance = jnp.sum(centred * centred, axis=-1, keepdims=True) * (1.0 / size)
+    normed = centred * lax.rsqrt(variance + EPS) * gain_ref[...] + shift_ref[...]
+    normed = normed.astype(LOWER)
+    n_ref[...] = normed
+    query = jnp.dot(normed, wq_ref[...], preferred_element_type=FLOAT) + bias_ref[0:1, :]
+    q_ref[...] = (query * HEAD_DIM ** (-0.5)).astype(LOWER)
+    k_ref[...] = jnp.dot(normed, wk_ref[...], preferred_element_type=FLOAT).astype(LOWER)
+    value = jnp.dot(normed, wv_ref[...], preferred_element_type=FLOAT) + bias_ref[1:2, :]
+    v_ref[...] = value.astype(LOWER)
+
+
+def project(joint, rows, gain, shift, bias, w_query, w_key, w_value):
+    pieces, _, model = joint.shape
+    width = w_query.shape[1]
+    whole = lambda i: (0, 0)
+    by_piece = lambda i: (i, 0)
+    weight = pl.BlockSpec((model, width), whole)
+    return pl.pallas_call(
+        project_kernel,
+        grid=(pieces,),
+        in_specs=[
+            pl.BlockSpec((1, rows, model), lambda i: (i, 0, 0)),
+            pl.BlockSpec((1, model), whole),
+            pl.BlockSpec((1, model), whole),
+            pl.BlockSpec((2, width), whole),
+            weight,
+            weight,
+            weight,
+        ],
+        out_specs=[pl.BlockSpec((rows, model), by_piece)]
+        + [pl.BlockSpec((rows, width), by_piece)] * 3,
+        out_shape=[jax.ShapeDtypeStruct((pieces * rows, model), LOWER)]
+        + [jax.ShapeDtypeStruct((pieces * rows, width), LOWER)] * 3,
+        compiler_params=pltpu.CompilerParams(vmem_limit_bytes=48 * 2**20),
+        cost_estimate=kernel_cost(12, pieces * rows, width),
+        name="project",
+    )(joint, gain, shift, bias, w_query, w_key, w_value)
 
 
 class Exchange:
@@ -292,50 +340,179 @@
     def flat(self):
         return lax.axis_index("seq") * self.heads + lax.axis_index("head")
 
-    def square_gather(self, block):
-        half = block.shape[0] // 2
-        from_side = self.send(block, self.side)
-        from_low = self.send(block, self.low)
+    def bit_swaps(self):
+        head_bits = [self.swap(0, 1 << b) for b in range(self.heads.bit_length() - 1)]
+        return head_bits + [self.swap(1 << b, 0) for b in range(self.seqs.bit_length() - 1)]
+
+    def row_gather(self, row):
+        size = row.shape[0]
+        for pairs in self.bit_swaps():
+            row = jnp.concatenate([row, self.send(row, pairs)])
+        count = self.seqs * self.heads
+        order = jnp.arange(count, dtype=jnp.int32) ^ self.flat()
+        return jnp.take(row.reshape(count, size), order, axis=0)
+
+    def row_scatter(self, rows):
+        rows = jnp.take(rows, jnp.arange(rows.shape[0], dtype=jnp.int32) ^ self.flat(), axis=0)
+        swaps = self.bit_swaps()
+        first = self.heads.bit_length() - 1
+        rows = rows.reshape(self.seqs, self.heads, -1).swapaxes(0, 1).reshape(rows.shape)
+        for pairs in swaps[:first][::-1] + swaps[first:][::-1]:
+            half = rows.shape[0] // 2
+            rows = rows[:half] + self.send(rows[half:], pairs)
+        return rows[0]
+
+    def seq_sum(self, value):
+        half = value.shape[0] // 2
+        swaps = [self.swap(1 << b, 0) for b in range(self.seqs.bit_length() - 1)]
+        first, second = value[:half], value[half:]
+        for one, two in zip(swaps, reversed(swaps)):
+            first = (first.astype(FLOAT) + self.send(first, one).astype(FLOAT)).astype(LOWER)
+            second = (second.astype(FLOAT) + self.send(second, two).astype(FLOAT)).astype(LOWER)
+        return jnp.concatenate([first, second])
+
+    def chip_orders(self):
+        bits = list(range(self.seqs.bit_length() - 1))
+        return bits, bits[::-1]
+
+    def double(self, part, other, bit):
+        mine = (lax.axis_index("seq") >> bit) & 1
+        return jnp.where(mine == 0, jnp.stack([part, other]), jnp.stack([other, part]))
+
+    def chip_send(self, pieces, step):
+        return [
+            self.send(piece, self.swap(1 << order[step], 0))
+            for order, piece in zip(self.chip_orders(), pieces)
+        ]
+
+    def chip_double(self, pieces, got, step):
+        return [
+            self.double(piece, other, order[step])
+            for order, piece, other in zip(self.chip_orders(), pieces, got)
+        ]
+
+    def chip_join(self, pieces):
+        sides = []
+        for order, piece in zip(self.chip_orders(), pieces):
+            at = [order[::-1].index(b) for b in sorted(order)[::-1]]
+            piece = jnp.transpose(piece, at + list(range(len(at), piece.ndim)))
+            sides.append(piece.reshape(-1, piece.shape[-1]))
+        return jnp.concatenate(sides, axis=-1)
+
+    def halves(self, part, at, size, mine):
+        shape = part.shape
+        split = part.reshape(shape[:at] + (shape[at] // (2 * size), 2, size) + shape[at + 1 :])
+        rest = shape[:at] + (shape[at] // 2,) + shape[at + 1 :]
+        keep = lax.dynamic_index_in_dim(split, mine, at + 1, keepdims=False).reshape(rest)
+        give = lax.dynamic_index_in_dim(split, 1 - mine, at + 1, keepdims=False).reshape(rest)
+        return keep, give
+
+    def scatter_start(self, value):
+        own = value.shape[0] // (self.seqs * self.heads)
+        part = value.reshape(self.seqs, self.heads, own, value.shape[1])
+        keep, give = self.halves(part, 1, 1, lax.axis_index("head") & 1)
+        return keep, self.send(give, self.core)
+
+    def scatter_sides(self, keep, got):
+        part = (keep.astype(FLOAT) + got.astype(FLOAT)).astype(LOWER)
+        width = part.shape[-1]
+        s = lax.axis_index("seq")
+        bits = list(range(self.seqs.bit_length() - 1))
+        state = []
+        for order, piece in (
+            (bits, part[..., : width // 2]),
+            (bits[::-1], part[..., width // 2 :]),
+        ):
+            b = order[0]
+            keep, give = self.halves(piece, 0, 1 << b, (s >> b) & 1)
+            state.append((keep, give, order))
+        return state
+
+    def scatter_end(self, state):
+        s, h = lax.axis_index("seq"), lax.axis_index("head")
+        sides = []
+        for keep, got, order in state:
+            left = list(order)
+            left.remove(order[0])
+            piece = (keep.astype(FLOAT) + got.astype(FLOAT)).astype(LOWER)
+            for b in order[1:]:
+                size = 1 << sorted(left).index(b)
+                keep, give = self.halves(piece, 0, size, (s >> b) & 1)
+                got = self.send(give, self.swap(1 << b, 0))
+                piece = (keep.astype(FLOAT) + got.astype(FLOAT)).astype(LOWER)
+                left.remove(b)
+            sides.append(piece)
+        part = jnp.concatenate(sides, axis=-1)
+        for b in range(1, self.heads.bit_length() - 1):
+            keep, give = self.halves(part, 1, 1, (h >> b) & 1)
+            got = self.send(give, self.swap(0, 1 << b))
+            part = (keep.astype(FLOAT) + got.astype(FLOAT)).astype(LOWER)
+        return part.reshape(-1, part.shape[-1]).astype(FLOAT)
+
+    def outer_sides(self, block):
+        return [self.send(block, self.back(i, 0)) for i in range(1, self.outer_seq)]
+
+    def outer_far(self, block, pieces=1):
+        size = block.shape[0] // pieces
+        gathered = []
+        for j in range(1, self.outer_head):
+            got = []
+            for p in range(pieces):
+                part = block[p * size : (p + 1) * size]
+                part = after(part, got[-1]) if got else part
+                got.append(self.send(part, self.back(0, j)))
+            gathered.append(jnp.concatenate(got) if pieces > 1 else got[0])
+        return gathered
+
+    def side_parts(self, parts):
+        return [
+            self.send(parts[j * self.outer_seq + i], self.ahead(i, 0))
+            for j in range(self.outer_head)
+            for i in range(1, self.outer_seq)
+        ]
+
+    def side_sums(self, parts, got):
+        sums = []
+        for j in range(self.outer_head):
+            here = parts[j * self.outer_seq].astype(FLOAT)
+            for i in range(self.outer_seq - 1):
+                here = here + got[j * (self.outer_seq - 1) + i].astype(FLOAT)
+            sums.append(here if j == 0 else here.astype(LOWER))
+        return sums
+
+    def far_parts(self, sums):
+        return [self.send(sums[j], self.ahead(0, j)) for j in range(1, self.outer_head)]
+
+    def far_sum(self, sums, got):
+        total = sums[0]
+        for one in got:
+            total = total + one.astype(FLOAT)
+        return total
+
+    def corner_gather(self, from_side, from_low):
+        half = from_side.shape[0] // 2
         first = self.send(from_side[:half], self.low)
         second = self.send(from_low[half:], self.side)
-        same = [block, from_side, from_low, jnp.concatenate([first, second])]
-        return same + [self.send(one, self.core) for one in same]
-
-    def square_scatter(self, parts):
-        same, other = parts[:4], parts[4:]
-        got = [self.send(one, self.core) for one in other]
-        total = [a.astype(FLOAT) + b.astype(FLOAT) for a, b in zip(same, got)]
+        return jnp.concatenate([first, second])
+
+    def core_sums(self, parts):
+        got = [self.send(one, self.core) for one in parts[4:]]
+        return [a.astype(FLOAT) + b.astype(FLOAT) for a, b in zip(parts[:4], got)]
+
+    def corner_sums(self, total):
         corner = total[3].astype(LOWER)
         half = corner.shape[0] // 2
         first = self.send(corner[:half], self.low).astype(FLOAT)
         second = self.send(corner[half:], self.side).astype(FLOAT)
         to_side = jnp.concatenate([total[1][:half] + first, total[1][half:]]).astype(LOWER)
         to_low = jnp.concatenate([total[2][:half], total[2][half:] + second]).astype(LOWER)
-        from_side = self.send(to_side, self.side).astype(FLOAT)
-        from_low = self.send(to_low, self.low).astype(FLOAT)
-        return total[0] + from_side + from_low
-
-    def outer_gather(self, block):
-        gathered = []
-        for j in range(self.outer_head):
-            here = block if j == 0 else self.send(block, self.back(0, j))
-            gathered += [
-                here if i == 0 else self.send(here, self.back(i, 0)) for i in range(self.outer_seq)
-            ]
-        return gathered
-
-    def outer_scatter(self, parts):
-        total = None
-        for j in range(self.outer_head):
-            mine = parts[j * self.outer_seq : (j + 1) * self.outer_seq]
-            here = mine[0].astype(FLOAT)
-            for i in range(1, self.outer_seq):
-                here = here + self.send(mine[i], self.ahead(i, 0)).astype(FLOAT)
-            if j == 0:
-                total = here
-            else:
-                total = total + self.send(here.astype(LOWER), self.ahead(0, j)).astype(FLOAT)
-        return total
+        return [total[0], to_side, to_low]
+
+    def near_parts(self, total):
+        return [self.send(total[1], self.side), self.send(total[2], self.low)]
+
+    def near_sums(self, total, got):
+        return total[0] + got[0].astype(FLOAT) + got[1].astype(FLOAT)
 
     def outer_owners(self):
         s, h = lax.axis_index("seq"), lax.axis_index("head")
@@ -378,7 +555,7 @@
     owners = net.outer_owners()
 
     small = jnp.concatenate([ln1_gain, ln1_bias, b_out, ln2_gain, ln2_bias, b_down, b_up])
-    small = lax.all_gather(small[None], both, axis=0, tiled=True)
+    small = net.row_gather(small)
     own = model // devices
 
     def vector(i):
@@ -389,48 +566,106 @@
         [lax.dynamic_slice(small, (d, 6 * own), (1, ff_width))[0] for d in owners]
     ).astype(FLOAT)
 
-    x_group = lax.all_gather(layer_input, "head", axis=0, tiled=True)
-    up_full = jnp.concatenate(net.outer_gather(w_up), axis=1)
-    down_full = jnp.concatenate(net.outer_gather(w_down), axis=0)
-    cot_group = jnp.concatenate(net.square_gather(cotangent), axis=0)
-    proj_out = lax.all_gather(w_out, both, axis=0, tiled=True)
-
-    normed_one = layer_norm(x_group.astype(FLOAT), gain_one, shift_one).astype(LOWER)
-    query = (
-        (jnp.dot(normed_one, w_query, preferred_element_type=FLOAT) + b_query.astype(FLOAT)) * scale
-    ).astype(LOWER)
-    keys = jnp.dot(normed_one, w_key, preferred_element_type=FLOAT).astype(LOWER)
-    values = (
-        jnp.dot(normed_one, w_value, preferred_element_type=FLOAT) + b_value.astype(FLOAT)
-    ).astype(LOWER)
+    core = lax.axis_index("head") & 1
+    up_near = [w_up] + net.outer_sides(w_up)
+    down_near = [w_down] + net.outer_sides(w_down)
+    joint = lax.all_gather(jnp.concatenate([layer_input, w_out]), "head", axis=0)
+    cot_side = net.send(cotangent, net.side)
+    joint = after(joint, small, cot_side, *up_near, *down_near)
+    out_mine = joint.reshape(net.heads // 2, 2, rows + own, model)[:, :, rows:]
+    out_mine = lax.dynamic_index_in_dim(out_mine, core, 1, keepdims=False)
+    out_pieces = [out_mine[..., : model // 2], out_mine[..., model // 2 :]]
+    steps = len(net.chip_orders()[0])
+    out_got = net.chip_send(out_pieces, 0)
+    up_far = net.outer_far(after(w_up, joint))
+    cot_low = net.send(after(cotangent, joint), net.low)
+    normed_one, query, keys, values = project(
+        joint,
+        rows,
+        gain_one[None],
+        shift_one[None],
+        jnp.stack([b_query, b_value]).astype(FLOAT),
+        w_query,
+        w_key,
+        w_value,
+    )
+    query = after(query, *out_got)
+    for step in range(1, steps):
+        out_pieces = net.chip_double(out_pieces, [after(one, query) for one in out_got], step - 1)
+        out_got = net.chip_send(out_pieces, step)
     counts = jnp.stack([mem_count, text_len, slot_count])
     context, context32, logsum = attention_forward(query, keys, values, counts)
+    context = after(context, cot_low, *out_got, *up_far)
+    out_pieces = net.chip_double(out_pieces, [after(one, context) for one in out_got], steps - 1)
+    out_half = net.chip_join(out_pieces)
+
     ctx_tok = lax.all_to_all(context, "head", split_axis=0, concat_axis=1, tiled=True)
+    cot_corner = net.corner_gather(after(cot_side, context), after(cot_low, context))
+    cot_same = [cotangent, cot_side, cot_low, cot_corner]
+    cot_blocks = cot_same + [net.send(after(one, context), net.core) for one in cot_same]
+    out_other = net.send(after(out_half, context), net.core)
+    up_blocks = list(up_near)
+    for one in up_far:
+        up_blocks += [one] + net.outer_sides(after(one, context))
+    down_far = net.outer_far(after(w_down, context), 2)
+    ctx_tok = after(ctx_tok, out_other, *up_blocks, *cot_blocks, *down_far)
 
     inputs_f = layer_input.astype(FLOAT)
-    hidden = inputs_f + (jnp.dot(ctx_tok, proj_out, preferred_element_type=FLOAT) + bias_out)
+    ctx_pairs = ctx_tok.reshape(rows, devices // 2, 2, own)
+    ctx_half = lax.dynamic_index_in_dim(ctx_pairs, core, 2, keepdims=False)
+    ctx_half = ctx_half.reshape(rows, model // 2)
+    ctx_other = lax.dynamic_index_in_dim(ctx_pairs, 1 - core, 2, keepdims=False)
+    ctx_other = ctx_other.reshape(rows, model // 2)
+    attended = jnp.dot(ctx_half, out_half, preferred_element_type=FLOAT)
+    attended = attended + jnp.dot(ctx_other, out_other, preferred_element_type=FLOAT)
+    hidden = inputs_f + (attended + bias_out)
     xhat_two, inverse_two = norm_parts(hidden)
     normed_two = (xhat_two * gain_two + shift_two).astype(LOWER)
 
-    n2_group = jnp.concatenate(net.square_gather(normed_two), axis=0)
+    cot_group = jnp.concatenate([after(one, normed_two) for one in cot_blocks], axis=0)
+    up_full = jnp.concatenate([after(one, normed_two) for one in up_blocks], axis=1)
+    n2_side, n2_low = net.send(normed_two, net.side), net.send(normed_two, net.low)
+    n2_same = [normed_two, n2_side, n2_low, net.corner_gather(n2_side, n2_low)]
+    n2_blocks = n2_same + [net.send(one, net.core) for one in n2_same]
+    n2_group = jnp.concatenate(n2_blocks, axis=0)
+    down_blocks = list(down_near)
+    for one in down_far:
+        down_blocks += [one] + net.outer_sides(after(one, ctx_tok))
+    n2_group = after(n2_group, *down_blocks)
+    down_full = jnp.concatenate([after(one, n2_side) for one in down_blocks], axis=0)
     pre_act = jnp.dot(n2_group, up_full, preferred_element_type=FLOAT) + bias_up
     act, slope = gelu_pair(pre_act)
     act = act.astype(LOWER)
-    grad_pre = (slope * cols_by_cols(cot_group, down_full)).astype(LOWER)
-    grad_n2_part = cols_by_cols(grad_pre, up_full).astype(LOWER)
-    grad_n2 = net.square_scatter([grad_n2_part[i * rows : (i + 1) * rows] for i in range(8)])
-    out_part = jnp.dot(act, down_full, preferred_element_type=FLOAT).astype(LOWER)
-    out_sum = net.square_scatter([out_part[i * rows : (i + 1) * rows] for i in range(8)])
-    output = (hidden + (out_sum + bias_down)).astype(LOWER)
     outer = len(owners)
     down_part = contract_rows(act, cot_group).astype(LOWER)
-    grad_w_down = net.outer_scatter(
-        [down_part[i * ff_width : (i + 1) * ff_width] for i in range(outer)]
-    )
-    up_part = contract_rows(n2_group, grad_pre).astype(LOWER)
-    grad_w_up = net.outer_scatter(
-        [up_part[:, i * ff_width : (i + 1) * ff_width] for i in range(outer)]
-    )
+    down_parts = [down_part[i * ff_width : (i + 1) * ff_width] for i in range(outer)]
+    down_got = net.side_parts(down_parts)
+    down_later = after(down_full, down_part)
+    out_part = jnp.dot(act, down_later, preferred_element_type=FLOAT).astype(LOWER)
+    sums_out = net.core_sums([out_part[i * rows : (i + 1) * rows] for i in range(8)])
+    grad_pre = (slope * cols_by_cols(after(cot_group, out_part), down_later)).astype(LOWER)
+    out_stage = net.corner_sums(sums_out)
+    out_near = net.near_parts(out_stage)
+    up_later = after(up_full, *down_got[1::2])
+    grad_n2_part = cols_by_cols(grad_pre, up_later).astype(LOWER)
+    sums_n2 = net.core_sums([grad_n2_part[i * rows : (i + 1) * rows] for i in range(8)])
+    up_part = contract_rows(n2_group, after(grad_pre, grad_n2_part, *out_stage[1:])).astype(LOWER)
+    sums_n2[3] = after(sums_n2[3], up_part, *out_near)
+    out_sum = net.near_sums(out_stage, out_near)
+    down_sums = net.side_sums(down_parts, down_got)
+    down_far_got = net.far_parts(down_sums)
+    n2_stage = net.corner_sums(sums_n2)
+    up_parts = [up_part[:, i * ff_width : (i + 1) * ff_width] for i in range(outer)]
+    up_got = net.side_parts(up_parts)
+    n2_stage[1] = after(n2_stage[1], *up_got[1::2], *down_far_got)
+    n2_stage[2] = after(n2_stage[2], n2_stage[1])
+    grad_n2 = net.near_sums(n2_stage, net.near_parts(n2_stage))
+    grad_n2 = after(grad_n2, *up_got[::2], *down_got[::2])
+    grad_w_down = net.far_sum(down_sums, [after(one, grad_n2) for one in down_far_got])
+    half = model // 2
+    up_sums = net.side_sums(up_parts, [after(one, grad_n2) for one in up_got])
+    up_halves = [[one[:half] for one in up_sums], [one[half:] for one in up_sums]]
+    up_far_got = net.far_parts(up_halves[0])
     b_up_part = jnp.sum(grad_pre.astype(FLOAT), 0)
 
     grad_out_f = cotangent.astype(FLOAT)
@@ -440,57 +675,86 @@
     grad_hidden = grad_out_f + norm_back(xhat_two, inverse_two, gain_two, grad_n2)
     grad_att = grad_hidden.astype(LOWER)
     b_out_part = jnp.sum(grad_att.astype(FLOAT), 0)
-    grad_ctx = cols_by_cols(grad_att, proj_out).astype(LOWER)
+    grad_ctx = jnp.stack(
+        [cols_by_cols(grad_att, one).reshape(rows, devices // 2, own) for one in (out_half, out_other)],
+        axis=2,
+    )
+    grad_ctx = jnp.where(core == 0, grad_ctx, grad_ctx[:, :, ::-1]).astype(LOWER)
+    grad_ctx = grad_ctx.reshape(rows, model)
     grad_heads = lax.all_to_all(grad_ctx, "head", split_axis=1, concat_axis=0, tiled=True)
-    grad_w_out = lax.psum_scatter(
-        contract_rows(ctx_tok, grad_att).astype(LOWER), both, scatter_dimension=0, tiled=True
-    ).astype(FLOAT)
+
+    out_keep, out_got = net.scatter_start(contract_rows(ctx_tok, grad_att).astype(LOWER))
+    out_state = net.scatter_sides(out_keep, out_got)
+    grad_heads = after(grad_heads, *up_far_got, *[give for _, give, _ in out_state])
+    up_far_late = net.far_parts([after(one, grad_heads) for one in up_halves[1]])
+    out_state = [(k, after(g, grad_heads), o) for k, g, o in out_state]
+    out_state = [(k, net.send(g, net.swap(1 << o[0], 0)), o) for k, g, o in out_state]
 
     grad_q, grad_k, grad_v = attention_backward(
         query, keys, values, context32, grad_heads, logsum, counts
     )
-    grad_n1_part = (
-        cols_by_cols(grad_q, w_query) + cols_by_cols(grad_k, w_key) + cols_by_cols(grad_v, w_value)
-    ).astype(LOWER)
+    grad_joined = jnp.concatenate([grad_q, grad_k, grad_v], axis=1)
+    out_raw = [got for _, got, _ in out_state]
+    grad_joined = after(grad_joined, *out_raw, *up_far_late)
+    output = (hidden + (out_sum + bias_down)).astype(LOWER)
+    out_state = [(k, after(g, grad_joined), o) for k, g, o in out_state]
+    grad_w_up = jnp.concatenate(
+        [
+            net.far_sum(sums, [after(one, grad_joined) for one in got])
+            for sums, got in zip(up_halves, (up_far_got, up_far_late))
+        ]
+    )
+    joined_w = jnp.concatenate([w_query, w_key, w_value], axis=1)
+    grad_n1_part = cols_by_cols(grad_joined, joined_w).astype(LOWER)
+    weight_part = contract_rows(normed_one, after(grad_joined, grad_n1_part)).astype(LOWER)
     grad_n1 = lax.psum_scatter(grad_n1_part, "head", scatter_dimension=0, tiled=True).astype(FLOAT)
-    weight_part = jnp.stack([contract_rows(normed_one, g) for g in (grad_q, grad_k, grad_v)])
-    weight_sum = lax.psum(weight_part.astype(LOWER), "seq").astype(FLOAT)
-    b_query_part = jnp.sum(grad_q.astype(FLOAT), 0)
-    b_value_part = jnp.sum(grad_v.astype(FLOAT), 0)
-
-    xhat_one, inverse_one = norm_parts(inputs_f)
-    gain_one_part = jnp.sum(grad_n1 * xhat_one, 0)
-    shift_one_part = jnp.sum(grad_n1, 0)
-    grad_input = (grad_hidden + norm_back(xhat_one, inverse_one, gain_one, grad_n1)).astype(LOWER)
-
-    row_of = jnp.arange(devices, dtype=jnp.int32)
     up_rows = jnp.zeros((devices, ff_width), FLOAT)
     for i, owner in enumerate(owners):
         up_rows = lax.dynamic_update_slice(
             up_rows, b_up_part[i * ff_width : (i + 1) * ff_width][None], (owner, 0)
         )
+    early_rows = (
+        jnp.concatenate(
+            [
+                part.reshape(devices, own)
+                for part in (b_out_part, gain_two_part, shift_two_part, b_down_part)
+            ]
+            + [up_rows],
+            axis=1,
+        )
+    )
+    early = net.row_scatter(after(early_rows, grad_n1_part))
+    weight_part = after(weight_part, early)
+    weight_sum = net.seq_sum(weight_part)
+    late_gate = weight_sum
+    weight_sum = weight_sum.astype(FLOAT)
+    weight_sum = [weight_sum[:, i * width : (i + 1) * width] for i in range(3)]
+    grad_w_out = net.scatter_end(out_state)
+    grad_n1 = after(grad_n1, *weight_sum, grad_w_up, grad_w_out)
+    b_query_part = jnp.sum(grad_q.astype(FLOAT), 0)
+    b_value_part = jnp.sum(grad_v.astype(FLOAT), 0)
+
+    xhat_one, inverse_one = norm_parts(inputs_f)
+    n1_part, x_group, _ = lax.optimization_barrier((grad_n1_part, joint, weight_part))
+    x_group = x_group[:, :rows].reshape(-1, model)
+    n1_part = n1_part.astype(FLOAT)
+    xhat_all, _ = norm_parts(x_group.astype(FLOAT))
+    gain_one_part = jnp.sum(n1_part * xhat_all, 0)
+    shift_one_part = jnp.sum(n1_part, 0)
+    grad_input = (grad_hidden + norm_back(xhat_one, inverse_one, gain_one, grad_n1)).astype(LOWER)
+
+    row_of = jnp.arange(devices, dtype=jnp.int32)
     mine = (row_of % net.heads == lax.axis_index("head"))[:, None]
     head_rows = jnp.where(mine, jnp.concatenate([b_query_part, b_value_part])[None], 0.0)
-    packed = jnp.concatenate(
-        [
-            part.reshape(devices, own)
-            for part in (
-                gain_one_part,
-                shift_one_part,
-                b_out_part,
-                gain_two_part,
-                shift_two_part,
-                b_down_part,
-            )
-        ]
-        + [up_rows, head_rows],
+    late_rows = jnp.concatenate(
+        [part.reshape(devices, own) for part in (gain_one_part, shift_one_part)] + [head_rows],
         axis=1,
     )
-    sums = lax.psum_scatter(packed, both, scatter_dimension=0, tiled=True)[0]
-    pieces = [sums[i * own : (i + 1) * own] for i in range(6)]
-    grad_b_up = sums[6 * own : 6 * own + ff_width]
-    grad_b_query = sums[6 * own + ff_width : 6 * own + ff_width + width]
-    grad_b_value = sums[6 * own + ff_width + width :]
+    late = net.row_scatter(after(late_rows, late_gate))
+    pieces = [late[:own], late[own : 2 * own]] + [early[i * own : (i + 1) * own] for i in range(4)]
+    grad_b_up = early[4 * own :]
+    grad_b_query = late[2 * own : 2 * own + width]
+    grad_b_value = late[2 * own + width :]
 
     return (
         output,

time: 1100 us -> 793 us (0.72)
  blocking collectives: 209 us -> 0 us
  waiting for transfers between devices: 504 us -> 340 us
  starting transfers between devices: 40.2 us -> 75.9 us
  matrix products: 138 us -> 111 us
  other arithmetic: 58.5 us -> 85.2 us
  Pallas kernels: 60.5 us -> 75.1 us
    all_gather x1 -> x0, blocking collectives: 178 us -> none  [body(): small = lax.all_gather(small[None], both, axis=0, tiled=True)]
    unnamed x7 -> x2, waiting for transfers between devices: 120 us -> 0.03 us
    reduce_scatter x1, waiting for transfers between devices: 88.2 us -> 0.01 us  [body(): lax.psum_scatter(grad_n1_part, 'head', scatter_dimension=0, tiled=True)]
    reduce_scatter x1 -> x0, waiting for transfers between devices: 53.2 us -> none  [body(): lax.psum_scatter(contract_rows(ctx_tok, grad_att).astype(LOWER), both, sc...]
    all_gather x2 -> x1, waiting for transfers between devices: 0.01 us -> 50.9 us  [body(): lax.all_gather(jnp.concatenate([layer_input, w_out]), 'head', axis=0)]
    ppermute x44 -> x77, starting transfers between devices: 36.2 us -> 68 us  [send(): return lax.ppermute(value, self.axes, pairs)]
    all_to_all x1 -> x0, blocking collectives: 31.4 us -> none  [body(): lax.all_to_all(grad_ctx, 'head', split_axis=1, concat_axis=0, tiled=True)]
    all_to_all x0 -> x1, waiting for transfers between devices: none -> 30.9 us  [body(): lax.all_to_all(grad_ctx, 'head', split_axis=1, concat_axis=0, tiled=True)]
  transfers between devices with their start and end apart: 51 -> 81, of which waited for: 17 -> 38; matrix products, arithmetic and copies ran while one was open for 17% -> 22% of each run, Pallas kernels for 2% -> 10%
where the time goes in v2:
time: 793 us; the launch traced here: 784 us
  waiting for transfers between devices  340 us (43%)
  matrix products  111 us (14%)
  other arithmetic  85.2 us (11%)
  local copies, waits for them, and re-layouts  77.8 us (10%)
  starting transfers between devices  75.9 us (10%)
  Pallas kernels  75.1 us (9%)
  between operations  18.4 us (2%)
    ppermute x77, waiting for transfers between devices, send(): return lax.ppermute(value, self.axes, pairs)  259 us
    ppermute x77, starting transfers between devices, send(): return lax.ppermute(value, self.axes, pairs)  68 us
    all_gather x1, waiting for transfers between devices, body(): lax.all_gather(jnp.concatenate([layer_input, w_out]), 'head', axis=0)  50.9 us
    dot_general x5, matrix products, cols_by_cols(): lax.dot_general(left, right, (((1,), (1,)), ((), ())), preferred_element_...  46.4 us
    unnamed x193, local copies, waits for them, and re-layouts  35.9 us
    pallas_call x1, Pallas kernels, attention_backward(): pl.pallas_call(backward_kernel, grid_spec=pltpu.PrefetchScalarGridSpec(nu...  33.6 us
    dot_general x4, matrix products, contract_rows(): lax.dot_general(left, right, (((0,), (0,)), ((), ())), preferred_element_...  33.1 us
    all_to_all x1, waiting for transfers between devices, body(): lax.all_to_all(grad_ctx, 'head', split_axis=1, concat_axis=0, tiled=True)  30.9 us
  transfers between devices with their start and end apart: 81, of which 38 were waited for; matrix products, arithmetic and copies ran while one was open for 22% of the time, Pallas kernels for 10%

profile of v2, /device:TPU:0, one launch (start us, length us, event | category | flops | bytes accessed | tf_op | source)
XLA Modules:
  0.0 783.8 jit_solution(17728773714225801901)
XLA Ops:
  9.9 3.0 collective-permute-start.5
  24.9 11.7 %collective-permute-done.3 = bf16[5120]{0:T(1024)(128)(2,1)S(1)} collective-permute-done((bf16[5120]{0:T(1024)(128)(2,1)S(1)}, bf16[5120]{0:T(1024)(128)(2,1)S(1)}, u32[]{:S(2)}, u32[]{:S(2)}) %collective-permute-start.3) | collective-permute-done | bytes 10272 | tf_op jit(solution)/shard_map/ppermute | solution.py:338
  38.4 22.3 %collective-permute-done.4 = bf16[10240]{0:T(1024)(128)(2,1)S(1)} collective-permute-done((bf16[10240]{0:T(1024)(128)(2,1)S(1)}, bf16[10240]{0:T(1024)(128)(2,1)S(1)}, u32[]{:S(2)}, u32[]{:S(2)}) %collective-permute-start.4) | collective-permute-done | bytes 20512 | tf_op jit(solution)/shard_map/ppermute | solution.py:338
  61.6 50.9 %all-gather.3.cloned.1.call-done = bf16[2560,2048]{1,0:T(8,128)(2,1)} async-done(((bf16[320,2048]{1,0:T(8,128)(2,1)}), bf16[2560,2048]{1,0:T(8,128)(2,1)}) %all-gather.3.cloned.1.call-update) | async-done | bytes 10485776 | tf_op jit(solution)/shard_map/all_gather | solution.py:572
  124.4 15.0 %project.1 = (bf16[2048,2048]{1,0:T(8,128)(2,1)}, bf16[2048,256]{1,0:T(8,128)(2,1)S(1)}, bf16[2048,256]{1,0:T(8,128)(2,1)S(1)}, bf16[2048,256]{1,0:T(8,128)(2,1)S(1)}) custom-call(bf16[8,320,2048]{2,1,0:T(8,128)(2,1)} %bitcast.149, f32[1,2048]{1,0:T(1,128)S(1)} %reshape.536.gain_ref, f32[1,2048]{1,0:T(1,128)S(1)} %reshape.537.shift_ref, ...), custom_call_target="tpu_custom_call" | custom-call | flops 12000000 | bytes 1000000 | tf_op jit(solution)/shard_map/project/pallas_call | solution.py:286
  139.4 3.2 maximum_select_fusion.2
  148.0 26.6 %attn_fwd.1 = (bf16[2048,256]{1,0:T(8,128)(2,1)S(1)}, f32[2048,256]{1,0:T(8,128)}, f32[8,2048]{1,0:T(8,128)S(1)}) custom-call(s32[3,1]{1,0:T(4,128)S(1)} %copy.65.count_ref, bf16[2048,256]{1,0:T(8,128)(2,1)S(1)} %get-tuple-element.91.q_ref, bf16[2048,256]{1,0:T(8,128)(2,1)S(1)} %get-tuple-element.92.k_ref, bf16[2048,256]{1,0:T(8,128)(2,1)S(1)} %get-tuple-element.93.v_ref), custom_call_target="tpu_custom_call" | custom-call | flops 26000000 | bytes 1000000 | tf_op jit(solution)/shard_map/attn_fwd/pallas_call | solution.py:103
  194.0 3.8 all-to-all-start
  200.4 13.5 %collective-permute-done.22 = bf16[128,2048]{1,0:T(8,128)(2,1)} collective-permute-done((bf16[128,2048]{1,0:T(8,128)(2,1)}, bf16[128,2048]{1,0:T(8,128)(2,1)}, u32[]{:S(2)}, u32[]{:S(2)}) %collective-permute-start.22) | collective-permute-done | bytes 524320 | tf_op jit(solution)/shard_map/ppermute | solution.py:338
  213.9 3.4 collective-permute-done.16
  220.5 37.8 %collective-permute-done.23 = bf16[128,2048]{1,0:T(8,128)(2,1)} collective-permute-done((bf16[128,2048]{1,0:T(8,128)(2,1)}, bf16[128,2048]{1,0:T(8,128)(2,1)}, u32[]{:S(2)}, u32[]{:S(2)}) %collective-permute-start.23) | collective-permute-done | bytes 524320 | tf_op jit(solution)/shard_map/ppermute | solution.py:338
  261.9 3.1 fusion.48
  265.1 3.7 fusion.64
  289.3 6.9 collective-permute-done.24
  303.5 6.3 collective-permute-done.26
  317.1 13.9 %multiply_convert_fusion = (bf16[2048,1024]{1,0:T(8,128)(2,1)S(1)}, f32[2048,1024]{1,0:T(8,128)}) fusion(f32[1024]{0:T(1024)S(1)} %maximum_convert_fusion, bf16[2048,2048]{1,0:T(8,128)(2,1)} %constant_dynamic-update-slice_fusion.4, bf16[2048,1024]{1,0:T(8,128)(2,1)S(1)} %constant_dynamic-update-slice_fusion.13), kind=kOutput, calls=%fused_computation.20 | convolution fusion | flops 8602517504 | bytes 25169920 | tf_op jit(solution)/shard_map/dot_general | solution.py:636
  331.0 10.0 %convolution_convert_fusion.4 = bf16[1024,2048]{1,0:T(8,128)(2,1)S(1)} fusion(bf16[2048,1024]{1,0:T(8,128)(2,1)S(1)} %get-tuple-element.252, bf16[2048,2048]{1,0:T(8,128)(2,1)S(1)} %constant_dynamic-update-slice_fusion.17), kind=kOutput, calls=%fused_computation.29 | convolution fusion | flops 8592031744 | bytes 16777216 | tf_op jit(solution)/shard_map/dot_general | solution.py:257
  344.1 10.7 %convolution_convert_fusion.3 = bf16[2048,2048]{1,0:T(8,128)(2,1)S(1)} fusion(bf16[2048,1024]{1,0:T(8,128)(2,1)} %copy-done.78, bf16[1024,2048]{1,0:T(8,128)(2,1)S(1)} %pad_maximum_fusion.1), kind=kOutput, calls=%fused_computation.25 | convolution fusion | flops 8594128896 | bytes 16777216 | tf_op jit(solution)/shard_map/dot_general | solution.py:644
  359.2 16.6 %convert_reduce_fusion.2 = (f32[1024]{0:T(1024)S(1)}, bf16[2048,1024]{1,0:T(8,128)(2,1)}) fusion(bf16[2048,2048]{1,0:T(8,128)(2,1)} %copy-done.66, bf16[1024,2048]{1,0:T(8,128)(2,1)S(1)} %pad_maximum_fusion.1, f32[2048,1024]{1,0:T(8,128)} %get-tuple-element.253, f32[1024]{0:T(1024)S(1)} %maximum_convert_fusion), kind=kOutput, calls=%fused_computation.19 | convolution fusion | flops 8617196544 | bytes 25174016 | tf_op jit(solution)/shard_map/dot_general | solution.py:19
  375.8 6.8 collective-permute-done.41
  382.5 14.1 %convolution_convert_fusion.2 = bf16[2048,2048]{1,0:T(8,128)(2,1)} fusion(bf16[2048,1024]{1,0:T(8,128)(2,1)} %get-tuple-element.132, bf16[2048,1024]{1,0:T(8,128)(2,1)} %copy-done.63), kind=kOutput, calls=%fused_computation.24 | convolution fusion | flops 8594128896 | bytes 16777216 | tf_op jit(solution)/shard_map/dot_general | solution.py:19
  396.6 3.5 fusion.49
  407.9 10.2 %collective-permute-done.36 = bf16[128,2048]{1,0:T(8,128)(2,1)S(1)} collective-permute-done((bf16[128,2048]{1,0:T(8,128)(2,1)S(1)}, bf16[128,2048]{1,0:T(8,128)(2,1)S(1)}, u32[]{:S(2)}, u32[]{:S(2)}) %collective-permute-start.36) | collective-permute-done | bytes 524320 | tf_op jit(solution)/shard_map/ppermute | solution.py:338
  421.1 11.4 %convolution_convert_fusion.5 = bf16[2048,1024]{1,0:T(8,128)(2,1)S(1)} fusion(bf16[2048,2048]{1,0:T(8,128)(2,1)S(1)} %bitcast.180, bf16[2048,1024]{1,0:T(8,128)(2,1)} %get-tuple-element.132), kind=kOutput, calls=%fused_computation.30 | convolution fusion | flops 8592031744 | bytes 16777216 | tf_op jit(solution)/shard_map/dot_general | solution.py:257
  436.6 6.5 collective-permute-done.37
  443.1 10.3 %collective-permute-done.40 = bf16[256,2048]{1,0:T(8,128)(2,1)S(1)} collective-permute-done((bf16[256,2048]{1,0:T(8,128)(2,1)S(1)}, bf16[256,2048]{1,0:T(8,128)(2,1)S(1)}, u32[]{:S(2)}, u32[]{:S(2)}) %collective-permute-start.40) | collective-permute-done | bytes 1048608 | tf_op jit(solution)/shard_map/ppermute | solution.py:338
  458.8 8.4 %collective-permute-done.50 = bf16[128,2048]{1,0:T(8,128)(2,1)S(1)} collective-permute-done((bf16[128,2048]{1,0:T(8,128)(2,1)S(1)}, bf16[128,2048]{1,0:T(8,128)(2,1)S(1)}, u32[]{:S(2)}, u32[]{:S(2)}) %collective-permute-start.50) | collective-permute-done | bytes 524320 | tf_op jit(solution)/shard_map/ppermute | solution.py:338
  467.1 9.7 %collective-permute-done.45 = bf16[128,2048]{1,0:T(8,128)(2,1)S(1)} collective-permute-done((bf16[128,2048]{1,0:T(8,128)(2,1)S(1)}, bf16[128,2048]{1,0:T(8,128)(2,1)S(1)}, u32[]{:S(2)}, u32[]{:S(2)}) %collective-permute-start.45) | collective-permute-done | bytes 524320 | tf_op jit(solution)/shard_map/ppermute | solution.py:338
  478.2 3.2 collective-permute-done.47
  485.2 21.2 %collective-permute-done.51 = bf16[256,2048]{1,0:T(8,128)(2,1)} collective-permute-done((bf16[256,2048]{1,0:T(8,128)(2,1)}, bf16[256,2048]{1,0:T(8,128)(2,1)}, u32[]{:S(2)}, u32[]{:S(2)}) %collective-permute-start.51) | collective-permute-done | bytes 1048608 | tf_op jit(solution)/shard_map/ppermute | solution.py:338
  509.4 19.8 %collective-permute-done.52 = bf16[2048,256]{1,0:T(8,128)(2,1)} collective-permute-done((bf16[2048,256]{1,0:T(8,128)(2,1)}, bf16[2048,256]{1,0:T(8,128)(2,1)}, u32[]{:S(2)}, u32[]{:S(2)}) %collective-permute-start.52) | collective-permute-done | bytes 1048608 | tf_op jit(solution)/shard_map/ppermute | solution.py:338
  530.3 4.9 convert_reduce_fusion.5
  545.3 3.5 fusion.65
  550.2 4.1 all-to-all-start.1
  554.4 3.7 convert_add_fusion.6
  561.8 30.9 %all-to-all-done.1 = bf16[256,8,256]{0,2,1:T(8,128)(2,1)S(1)} async-done(((bf16[256,8,256]{0,2,1:T(8,128)(2,1)}), bf16[256,8,256]{0,2,1:T(8,128)(2,1)S(1)}, u32[]{:S(2)}, u32[]{:S(2)}) %all-to-all-start.1) | async-done | bytes 1048608 | tf_op jit(solution)/shard_map/all_to_all | solution.py:684
  594.1 5.4 fusion.8
  600.2 3.2 collective-permute-done.54
  606.6 33.6 %attn_bwd.1 = (bf16[2048,256]{1,0:T(8,128)(2,1)S(1)}, bf16[2048,256]{1,0:T(8,128)(2,1)S(1)}, bf16[2048,256]{1,0:T(8,128)(2,1)S(1)}) custom-call(s32[3,1]{1,0:T(4,128)S(1)} %copy.65.count_ref, bf16[2048,256]{1,0:T(8,128)(2,1)S(1)} %copy-done.1, bf16[2048,256]{1,0:T(8,128)(2,1)S(1)} %copy-done.3, bf16[2048,256]{1,0:T(8,128)(2,1)} %copy-done.4, ...), custom_call_target="tpu_custom_call" | custom-call | flops 34000000 | bytes 1000000 | tf_op jit(solution)/shard_map/attn_bwd/pallas_call | solution.py:203
  643.8 9.4 %convolution_convert_fusion = bf16[2048,2048]{1,0:T(8,128)(2,1)} fusion(bf16[2048,768]{1,0:T(8,128)(2,1)S(1)} %pad_maximum_fusion.2, bf16[2048,256]{1,0:T(8,128)(2,1)S(1)} %copy-done.46, bf16[2048,256]{1,0:T(8,128)(2,1)S(1)} %copy-done.8, bf16[2048,256]{1,0:T(8,128)(2,1)S(1)} %copy-done.6), kind=kOutput, calls=%fused_computation.22 | convolution fusion | flops 6456082432 | bytes 14680064 | tf_op jit(solution)/shard_map/dot_general | solution.py:19
  654.6 3.9 convert_add_fusion.5
  659.2 9.4 %convolution_convert_fusion.6 = bf16[2048,768]{1,0:T(8,128)(2,1)S(1)} fusion(bf16[2048,2048]{1,0:T(8,128)(2,1)} %get-tuple-element.148, bf16[2048,768]{1,0:T(8,128)(2,1)S(1)} %copy-done.36), kind=kOutput, calls=%fused_computation.31 | convolution fusion | flops 6444023808 | bytes 14680064 | tf_op jit(solution)/shard_map/dot_general | solution.py:257
  680.2 4.7 fusion
  693.0 3.0 collective-permute-done.72
  696.1 3.0 pad_maximum_fusion.5
  704.0 6.3 collective-permute-done.75
  734.5 18.2 %collective-permute-done.65 = bf16[1,2,64,2048]{3,2,1,0:T(8,128)(2,1)S(1)} collective-permute-done((bf16[1,2,64,2048]{3,2,1,0:T(8,128)(2,1)S(1)}, bf16[1,2,64,2048]{3,2,1,0:T(8,128)(2,1)S(1)}, u32[]{:S(2)}, u32[]{:S(2)}) %collective-permute-start.65) | collective-permute-done | bytes 524320 | tf_op jit(solution)/shard_map/ppermute | solution.py:338
  756.2 10.7 %collective-permute-done.66 = bf16[1,1,64,2048]{3,2,1,0:T(8,128)(2,1)S(1)} collective-permute-done((bf16[1,1,64,2048]{3,2,1,0:T(8,128)(2,1)S(1)}, bf16[1,1,64,2048]{3,2,1,0:T(8,128)(2,1)S(1)}, u32[]{:S(2)}, u32[]{:S(2)}) %collective-permute-start.66) | collective-permute-done | bytes 262176 | tf_op jit(solution)/shard_map/ppermute | solution.py:338
  (512 shorter events, 220.7 us)
Async XLA Ops:
  7.3 105.2 %all-gather.3.cloned.1.call-start = ((), (), s32[]{:S(2)}) async-start(), calls=%async_computation.4 | async-start | bytes 11796480 | tf_op jit(solution)/shard_map/all_gather | solution.py:572
  9.9 51.6 %collective-permute-start.5 = (bf16[256,2048]{1,0:T(8,128)(2,1)}, bf16[256,2048]{1,0:T(8,128)(2,1)S(1)}, u32[]{:S(2)}, u32[]{:S(2)}) collective-permute-start(bf16[256,2048]{1,0:T(8,128)(2,1)} %param.39), channel_id=1, source_target_pairs={{0,8},{1,9},{2,10},{3,11},{4,12},{5,13},{6,14},{7,15},{8,0},{9,1},... | collective-permute-start | bytes 3145736 | tf_op jit(solution)/shard_map/ppermute | solution.py:338
  12.9 48.6 %collective-permute-start.6 = (bf16[2048,256]{1,0:T(8,128)(2,1)}, bf16[2048,256]{1,0:T(8,128)(2,1)S(1)}, u32[]{:S(2)}, u32[]{:S(2)}) collective-permute-start(bf16[2048,256]{1,0:T(8,128)(2,1)} %param.35), channel_id=1, source_target_pairs={{16,0},{17,1},{18,2},{19,3},{20,4},{21,5},{22,6},{23,7},{24,8},{25... | collective-permute-start | bytes 3145736 | tf_op jit(solution)/shard_map/ppermute | solution.py:338
  14.5 47.1 %collective-permute-start.7 = (bf16[256,2048]{1,0:T(8,128)(2,1)S(1)}, bf16[256,2048]{1,0:T(8,128)(2,1)}, u32[]{:S(2)}, u32[]{:S(2)}) collective-permute-start(bf16[256,2048]{1,0:T(8,128)(2,1)S(1)} %copy-done.32), channel_id=1, source_target_pairs={{16,0},{17,1},{18,2},{19,3},{20,4},{21,5},{22,6},{23,7},{24,8},{25... | collective-permute-start | bytes 3145736 | tf_op jit(solution)/shard_map/ppermute | solution.py:338
  120.6 57.3 %collective-permute-start.10 = (bf16[256,2048]{1,0:T(8,128)(2,1)}, bf16[256,2048]{1,0:T(8,128)(2,1)}, u32[]{:S(2)}, u32[]{:S(2)}) collective-permute-start(bf16[256,2048]{1,0:T(8,128)(2,1)} %param.39), channel_id=1, source_target_pairs={{0,2},{1,3},{2,0},{3,1},{4,6},{5,7},{6,4},{7,5},{8,10},{9,11},{10,... | collective-permute-start | bytes 3145736 | tf_op jit(solution)/shard_map/ppermute | solution.py:338
  120.6 57.2 %collective-permute-start.13 = (bf16[2048,256]{1,0:T(8,128)(2,1)}, bf16[2048,256]{1,0:T(8,128)(2,1)}, u32[]{:S(2)}, u32[]{:S(2)}) collective-permute-start(bf16[2048,256]{1,0:T(8,128)(2,1)} %param.35), channel_id=1, source_target_pairs={{4,0},{5,1},{6,2},{7,3},{0,4},{1,5},{2,6},{3,7},{12,8},{13,9},{14,... | collective-permute-start | bytes 3145736 | tf_op jit(solution)/shard_map/ppermute | solution.py:338
  142.6 35.3 %collective-permute-start.11 = (bf16[2,4,64,1024]{3,2,1,0:T(8,128)(2,1)}, bf16[2,4,64,1024]{3,2,1,0:T(8,128)(2,1)}, u32[]{:S(2)}, u32[]{:S(2)}) collective-permute-start(bf16[2,4,64,1024]{3,2,1,0:T(8,128)(2,1)} %maximum_select_fusion.2), channel_id=1, source_target_pairs={{0,16},{1,17},{2,18},{3,19},{4,20},{5,21},{6,22},{7,23},{8,24},{9,... | collective-permute-start | bytes 3145736 | tf_op jit(solution)/shard_map/ppermute | solution.py:338
  145.5 32.3 %collective-permute-start.12 = (bf16[2,4,64,1024]{3,2,1,0:T(8,128)(2,1)}, bf16[2,4,64,1024]{3,2,1,0:T(8,128)(2,1)}, u32[]{:S(2)}, u32[]{:S(2)}) collective-permute-start(bf16[2,4,64,1024]{3,2,1,0:T(8,128)(2,1)} %maximum_select_fusion.3), channel_id=1, source_target_pairs={{0,8},{1,9},{2,10},{3,11},{4,12},{5,13},{6,14},{7,15},{8,0},{9,1},... | collective-permute-start | bytes 3145736 | tf_op jit(solution)/shard_map/ppermute | solution.py:338
  185.5 76.3 %collective-permute-start.14 = (bf16[1024,2048]{1,0:T(8,128)(2,1)}, bf16[1024,2048]{1,0:T(8,128)(2,1)}, u32[]{:S(2)}, u32[]{:S(2)}) collective-permute-start(bf16[1024,2048]{1,0:T(8,128)(2,1)} %pad_maximum_fusion), channel_id=1, source_target_pairs={{0,1},{1,0},{2,3},{3,2},{4,5},{5,4},{6,7},{7,6},{8,9},{9,8},{10,11... | collective-permute-start | bytes 12582920 | tf_op jit(solution)/shard_map/ppermute | solution.py:338
  186.6 27.3 %collective-permute-start.22 = (bf16[128,2048]{1,0:T(8,128)(2,1)}, bf16[128,2048]{1,0:T(8,128)(2,1)}, u32[]{:S(2)}, u32[]{:S(2)}) collective-permute-start(bf16[128,2048]{1,0:T(8,128)(2,1)} %get-tuple-element.219), channel_id=1, source_target_pairs={{4,0},{5,1},{6,2},{7,3},{0,4},{1,5},{2,6},{3,7},{12,8},{13,9},{14,... | collective-permute-start | bytes 1572872 | tf_op jit(solution)/shard_map/ppermute | solution.py:338
  188.4 32.1 %collective-permute-start.15 = (bf16[2048,256]{1,0:T(8,128)(2,1)}, bf16[2048,256]{1,0:T(8,128)(2,1)}, u32[]{:S(2)}, u32[]{:S(2)}) collective-permute-start(bf16[2048,256]{1,0:T(8,128)(2,1)} %collective-permute-done.13), channel_id=1, source_target_pairs={{16,0},{17,1},{18,2},{19,3},{20,4},{21,5},{22,6},{23,7},{24,8},{25... | collective-permute-start | bytes 3145736 | tf_op jit(solution)/shard_map/ppermute | solution.py:338
  190.7 26.6 %collective-permute-start.16 = (bf16[128,2048]{1,0:T(8,128)(2,1)}, bf16[128,2048]{1,0:T(8,128)(2,1)}, u32[]{:S(2)}, u32[]{:S(2)}) collective-permute-start(bf16[128,2048]{1,0:T(8,128)(2,1)} %slice.336), channel_id=1, source_target_pairs={{0,2},{1,3},{2,0},{3,1},{4,6},{5,7},{6,4},{7,5},{8,10},{9,11},{10,... | collective-permute-start | bytes 1572872 | tf_op jit(solution)/shard_map/ppermute | solution.py:338
  194.0 67.8 %all-to-all-start = ((bf16[8,256,256]{1,2,0:T(8,128)(2,1)}), bf16[8,256,256]{1,2,0:T(8,128)(2,1)S(1)}, u32[]{:S(2)}, u32[]{:S(2)}) async-start(bf16[8,256,256]{1,2,0:T(8,128)(2,1)} %copy.66), calls=%async_computation | async-start | bytes 2097152 | tf_op jit(solution)/shard_map/all_to_all | solution.py:602
  213.9 44.5 %collective-permute-start.23 = (bf16[128,2048]{1,0:T(8,128)(2,1)}, bf16[128,2048]{1,0:T(8,128)(2,1)}, u32[]{:S(2)}, u32[]{:S(2)}) collective-permute-start(bf16[128,2048]{1,0:T(8,128)(2,1)} %get-tuple-element.109), channel_id=1, source_target_pairs={{4,0},{5,1},{6,2},{7,3},{0,4},{1,5},{2,6},{3,7},{12,8},{13,9},{14,... | collective-permute-start | bytes 1572872 | tf_op jit(solution)/shard_map/ppermute | solution.py:338
  217.3 43.5 %collective-permute-start.19 = (bf16[256,2048]{1,0:T(8,128)(2,1)}, bf16[256,2048]{1,0:T(8,128)(2,1)}, u32[]{:S(2)}, u32[]{:S(2)}) collective-permute-start(bf16[256,2048]{1,0:T(8,128)(2,1)} %copy-done.37), channel_id=1, source_target_pairs={{0,1},{1,0},{2,3},{3,2},{4,5},{5,4},{6,7},{7,6},{8,9},{9,8},{10,11... | collective-permute-start | bytes 3145736 | tf_op jit(solution)/shard_map/ppermute | solution.py:338
  219.2 41.6 %collective-permute-start.20 = (bf16[256,2048]{1,0:T(8,128)(2,1)}, bf16[256,2048]{1,0:T(8,128)(2,1)}, u32[]{:S(2)}, u32[]{:S(2)}) collective-permute-start(bf16[256,2048]{1,0:T(8,128)(2,1)} %collective-permute-done.10), channel_id=1, source_target_pairs={{0,1},{1,0},{2,3},{3,2},{4,5},{5,4},{6,7},{7,6},{8,9},{9,8},{10,11... | collective-permute-start | bytes 3145736 | tf_op jit(solution)/shard_map/ppermute | solution.py:338
  220.5 40.3 %collective-permute-start.18 = (bf16[256,2048]{1,0:T(8,128)(2,1)}, bf16[256,2048]{1,0:T(8,128)(2,1)}, u32[]{:S(2)}, u32[]{:S(2)}) collective-permute-start(bf16[256,2048]{1,0:T(8,128)(2,1)} %param.39), channel_id=1, source_target_pairs={{0,1},{1,0},{2,3},{3,2},{4,5},{5,4},{6,7},{7,6},{8,9},{9,8},{10,11... | collective-permute-start | bytes 3145736 | tf_op jit(solution)/shard_map/ppermute | solution.py:338
  270.6 25.6 %collective-permute-start.24 = (bf16[256,2048]{1,0:T(8,128)(2,1)S(1)}, bf16[256,2048]{1,0:T(8,128)(2,1)S(1)}, u32[]{:S(2)}, u32[]{:S(2)}) collective-permute-start(bf16[256,2048]{1,0:T(8,128)(2,1)S(1)} %get-tuple-element.177), channel_id=1, source_target_pairs={{0,8},{1,9},{2,10},{3,11},{4,12},{5,13},{6,14},{7,15},{8,0},{9,1},... | collective-permute-start | bytes 3145736 | tf_op jit(solution)/shard_map/ppermute | solution.py:338
  272.3 25.3 %collective-permute-start.25 = (bf16[256,2048]{1,0:T(8,128)(2,1)S(1)}, bf16[256,2048]{1,0:T(8,128)(2,1)S(1)}, u32[]{:S(2)}, u32[]{:S(2)}) collective-permute-start(bf16[256,2048]{1,0:T(8,128)(2,1)S(1)} %get-tuple-element.177), channel_id=1, source_target_pairs={{0,2},{1,3},{2,0},{3,1},{4,6},{5,7},{6,4},{7,5},{8,10},{9,11},{10,... | collective-permute-start | bytes 3145736 | tf_op jit(solution)/shard_map/ppermute | solution.py:338
  272.3 40.5 %collective-permute-start.28 = (bf16[256,2048]{1,0:T(8,128)(2,1)S(1)}, bf16[256,2048]{1,0:T(8,128)(2,1)S(1)}, u32[]{:S(2)}, u32[]{:S(2)}) collective-permute-start(bf16[256,2048]{1,0:T(8,128)(2,1)S(1)} %get-tuple-element.177), channel_id=1, source_target_pairs={{0,1},{1,0},{2,3},{3,2},{4,5},{5,4},{6,7},{7,6},{8,9},{9,8},{10,11... | collective-permute-start | bytes 3145736 | tf_op jit(solution)/shard_map/ppermute | solution.py:338
  273.8 25.4 %collective-permute-start.32 = (bf16[256,2048]{1,0:T(8,128)(2,1)S(1)}, bf16[256,2048]{1,0:T(8,128)(2,1)S(1)}, u32[]{:S(2)}, u32[]{:S(2)}) collective-permute-start(bf16[256,2048]{1,0:T(8,128)(2,1)S(1)} %copy-done.41), channel_id=1, source_target_pairs={{16,0},{17,1},{18,2},{19,3},{20,4},{21,5},{22,6},{23,7},{24,8},{25... | collective-permute-start | bytes 3145736 | tf_op jit(solution)/shard_map/ppermute | solution.py:338
  357.0 25.6 %collective-permute-start.41 = (bf16[256,2048]{1,0:T(8,128)(2,1)S(1)}, bf16[256,2048]{1,0:T(8,128)(2,1)S(1)}, u32[]{:S(2)}, u32[]{:S(2)}) collective-permute-start(bf16[256,2048]{1,0:T(8,128)(2,1)S(1)} %get-tuple-element.199), channel_id=1, source_target_pairs={{0,16},{1,17},{2,18},{3,19},{4,20},{5,21},{6,22},{7,23},{8,24},{9,... | collective-permute-start | bytes 3145736 | tf_op jit(solution)/shard_map/ppermute | solution.py:338
  358.5 42.2 %collective-permute-start.34 = (bf16[256,2048]{1,0:T(8,128)(2,1)}, bf16[256,2048]{1,0:T(8,128)(2,1)}, u32[]{:S(2)}, u32[]{:S(2)}) collective-permute-start(bf16[256,2048]{1,0:T(8,128)(2,1)} %get-tuple-element.187), channel_id=1, source_target_pairs={{0,1},{1,0},{2,3},{3,2},{4,5},{5,4},{6,7},{7,6},{8,9},{9,8},{10,11... | collective-permute-start | bytes 3145736 | tf_op jit(solution)/shard_map/ppermute | solution.py:338
  358.7 42.0 %collective-permute-start.38 = (bf16[256,2048]{1,0:T(8,128)(2,1)}, bf16[256,2048]{1,0:T(8,128)(2,1)}, u32[]{:S(2)}, u32[]{:S(2)}) collective-permute-start(bf16[256,2048]{1,0:T(8,128)(2,1)} %get-tuple-element.185), channel_id=1, source_target_pairs={{0,1},{1,0},{2,3},{3,2},{4,5},{5,4},{6,7},{7,6},{8,9},{9,8},{10,11... | collective-permute-start | bytes 3145736 | tf_op jit(solution)/shard_map/ppermute | solution.py:338
  359.0 41.7 %collective-permute-start.35 = (bf16[256,2048]{1,0:T(8,128)(2,1)}, bf16[256,2048]{1,0:T(8,128)(2,1)}, u32[]{:S(2)}, u32[]{:S(2)}) collective-permute-start(bf16[256,2048]{1,0:T(8,128)(2,1)} %get-tuple-element.186), channel_id=1, source_target_pairs={{0,1},{1,0},{2,3},{3,2},{4,5},{5,4},{6,7},{7,6},{8,9},{9,8},{10,11... | collective-permute-start | bytes 3145736 | tf_op jit(solution)/shard_map/ppermute | solution.py:338
  400.1 54.9 %collective-permute-start.43 = (bf16[256,2048]{1,0:T(8,128)(2,1)S(1)}, bf16[256,2048]{1,0:T(8,128)(2,1)S(1)}, u32[]{:S(2)}, u32[]{:S(2)}) collective-permute-start(bf16[256,2048]{1,0:T(8,128)(2,1)S(1)} %get-tuple-element.181), channel_id=1, source_target_pairs={{0,1},{1,0},{2,3},{3,2},{4,5},{5,4},{6,7},{7,6},{8,9},{9,8},{10,11... | collective-permute-start | bytes 3145736 | tf_op jit(solution)/shard_map/ppermute | solution.py:338
  400.1 56.3 %collective-permute-start.49 = (bf16[256,2048]{1,0:T(8,128)(2,1)S(1)}, bf16[256,2048]{1,0:T(8,128)(2,1)S(1)}, u32[]{:S(2)}, u32[]{:S(2)}) collective-permute-start(bf16[256,2048]{1,0:T(8,128)(2,1)S(1)} %get-tuple-element.179), channel_id=1, source_target_pairs={{0,1},{1,0},{2,3},{3,2},{4,5},{5,4},{6,7},{7,6},{8,9},{9,8},{10,11... | collective-permute-start | bytes 3145736 | tf_op jit(solution)/shard_map/ppermute | solution.py:338
  400.6 33.1 %collective-permute-start.44 = (bf16[256,2048]{1,0:T(8,128)(2,1)S(1)}, bf16[256,2048]{1,0:T(8,128)(2,1)S(1)}, u32[]{:S(2)}, u32[]{:S(2)}) collective-permute-start(bf16[256,2048]{1,0:T(8,128)(2,1)S(1)} %get-tuple-element.180), channel_id=1, source_target_pairs={{0,1},{1,0},{2,3},{3,2},{4,5},{5,4},{6,7},{7,6},{8,9},{9,8},{10,11... | collective-permute-start | bytes 3145736 | tf_op jit(solution)/shard_map/ppermute | solution.py:338
  418.3 24.8 %collective-permute-start.37 = (bf16[256,2048]{1,0:T(8,128)(2,1)S(1)}, bf16[256,2048]{1,0:T(8,128)(2,1)S(1)}, u32[]{:S(2)}, u32[]{:S(2)}) collective-permute-start(bf16[256,2048]{1,0:T(8,128)(2,1)S(1)} %pad_maximum_fusion.8), channel_id=1, source_target_pairs={{0,8},{1,9},{2,10},{3,11},{4,12},{5,13},{6,14},{7,15},{8,0},{9,1},... | collective-permute-start | bytes 3145736 | tf_op jit(solution)/shard_map/ppermute | solution.py:338
  419.3 34.2 %collective-permute-start.40 = (bf16[256,2048]{1,0:T(8,128)(2,1)S(1)}, bf16[256,2048]{1,0:T(8,128)(2,1)S(1)}, u32[]{:S(2)}, u32[]{:S(2)}) collective-permute-start(bf16[256,2048]{1,0:T(8,128)(2,1)S(1)} %pad_maximum_fusion.9), channel_id=1, source_target_pairs={{0,2},{1,3},{2,0},{3,1},{4,6},{5,7},{6,4},{7,5},{8,10},{9,11},{10,... | collective-permute-start | bytes 3145736 | tf_op jit(solution)/shard_map/ppermute | solution.py:338
  433.8 47.6 %collective-permute-start.47 = (bf16[256,2048]{1,0:T(8,128)(2,1)S(1)}, bf16[256,2048]{1,0:T(8,128)(2,1)S(1)}, u32[]{:S(2)}, u32[]{:S(2)}) collective-permute-start(bf16[256,2048]{1,0:T(8,128)(2,1)S(1)} %add_convert_fusion.5), channel_id=1, source_target_pairs={{0,4},{1,5},{2,6},{3,7},{4,0},{5,1},{6,2},{7,3},{8,12},{9,13},{10,... | collective-permute-start | bytes 3145736 | tf_op jit(solution)/shard_map/ppermute | solution.py:338
  443.1 42.1 %collective-permute-start.42 = (bf16[256,2048]{1,0:T(8,128)(2,1)}, bf16[256,2048]{1,0:T(8,128)(2,1)}, u32[]{:S(2)}, u32[]{:S(2)}) collective-permute-start(bf16[256,2048]{1,0:T(8,128)(2,1)} %get-tuple-element.178), channel_id=1, source_target_pairs={{0,1},{1,0},{2,3},{3,2},{4,5},{5,4},{6,7},{7,6},{8,9},{9,8},{10,11... | collective-permute-start | bytes 3145736 | tf_op jit(solution)/shard_map/ppermute | solution.py:338
  453.5 28.0 %collective-permute-start.46 = (bf16[2048,256]{1,0:T(8,128)(2,1)S(1)}, bf16[2048,256]{1,0:T(8,128)(2,1)S(1)}, u32[]{:S(2)}, u32[]{:S(2)}) collective-permute-start(bf16[2048,256]{1,0:T(8,128)(2,1)S(1)} %get-tuple-element.201), channel_id=1, source_target_pairs={{0,16},{1,17},{2,18},{3,19},{4,20},{5,21},{6,22},{7,23},{8,24},{9,... | collective-permute-start | bytes 3145736 | tf_op jit(solution)/shard_map/ppermute | solution.py:338
  483.1 26.3 %collective-permute-start.53 = (bf16[256,2048]{1,0:T(8,128)(2,1)}, bf16[256,2048]{1,0:T(8,128)(2,1)S(1)}, u32[]{:S(2)}, u32[]{:S(2)}) collective-permute-start(bf16[256,2048]{1,0:T(8,128)(2,1)} %get-tuple-element.198), channel_id=1, source_target_pairs={{0,16},{1,17},{2,18},{3,19},{4,20},{5,21},{6,22},{7,23},{8,24},{9,... | collective-permute-start | bytes 3145736 | tf_op jit(solution)/shard_map/ppermute | solution.py:338
  484.8 44.4 %collective-permute-start.52 = (bf16[2048,256]{1,0:T(8,128)(2,1)}, bf16[2048,256]{1,0:T(8,128)(2,1)}, u32[]{:S(2)}, u32[]{:S(2)}) collective-permute-start(bf16[2048,256]{1,0:T(8,128)(2,1)} %get-tuple-element.200), channel_id=1, source_target_pairs={{0,16},{1,17},{2,18},{3,19},{4,20},{5,21},{6,22},{7,23},{8,24},{9,... | collective-permute-start | bytes 3145736 | tf_op jit(solution)/shard_map/ppermute | solution.py:338
  485.2 45.1 %collective-permute-start.33 = (bf16[256,2048]{1,0:T(8,128)(2,1)}, bf16[256,2048]{1,0:T(8,128)(2,1)S(1)}, u32[]{:S(2)}, u32[]{:S(2)}) collective-permute-start(bf16[256,2048]{1,0:T(8,128)(2,1)} %get-tuple-element.184), channel_id=1, source_target_pairs={{0,1},{1,0},{2,3},{3,2},{4,5},{5,4},{6,7},{7,6},{8,9},{9,8},{10,11... | collective-permute-start | bytes 3145736 | tf_op jit(solution)/shard_map/ppermute | solution.py:338
  542.3 51.7 %collective-permute-start.55 = (bf16[4,4,64,2048]{3,2,1,0:T(8,128)(2,1)}, bf16[4,4,64,2048]{3,2,1,0:T(8,128)(2,1)}, u32[]{:S(2)}, u32[]{:S(2)}) collective-permute-start(bf16[4,4,64,2048]{3,2,1,0:T(8,128)(2,1)} %dynamic-slice_bitcast_fusion), channel_id=1, source_target_pairs={{0,1},{1,0},{2,3},{3,2},{4,5},{5,4},{6,7},{7,6},{8,9},{9,8},{10,11... | collective-permute-start | bytes 12582920 | tf_op jit(solution)/shard_map/ppermute | solution.py:338
  550.2 42.4 %all-to-all-start.1 = ((bf16[256,8,256]{0,2,1:T(8,128)(2,1)}), bf16[256,8,256]{0,2,1:T(8,128)(2,1)S(1)}, u32[]{:S(2)}, u32[]{:S(2)}) async-start(bf16[256,8,256]{0,2,1:T(8,128)(2,1)} %bitcast.30), calls=%async_computation.1 | async-start | bytes 2097152 | tf_op jit(solution)/shard_map/all_to_all | solution.py:684
  554.3 218.0 %reduce-scatter.2.cloned.1.call-start = ((), (), s32[]{:S(2)}) async-start(), calls=%async_computation.3 | async-start | bytes 9437184 | tf_op jit(solution)/shard_map/reduce_scatter | solution.py:710
  558.9 44.5 %collective-permute-start.54 = (bf16[1024,256]{1,0:T(8,128)(2,1)S(1)}, bf16[1024,256]{1,0:T(8,128)(2,1)S(1)}, u32[]{:S(2)}, u32[]{:S(2)}) collective-permute-start(bf16[1024,256]{1,0:T(8,128)(2,1)S(1)} %get-tuple-element.211), channel_id=1, source_target_pairs={{0,4},{1,5},{2,6},{3,7},{4,0},{5,1},{6,2},{7,3},{8,12},{9,13},{10,... | collective-permute-start | bytes 1572872 | tf_op jit(solution)/shard_map/ppermute | solution.py:338
  603.4 37.2 %collective-permute-start.56 = (bf16[2,4,64,1024]{3,2,1,0:T(8,128)(2,1)S(1)}, bf16[2,4,64,1024]{3,2,1,0:T(8,128)(2,1)S(1)}, u32[]{:S(2)}, u32[]{:S(2)}) collective-permute-start(bf16[2,4,64,1024]{3,2,1,0:T(8,128)(2,1)S(1)} %dynamic-slice_bitcast_fusion.2), channel_id=1, source_target_pairs={{0,8},{1,9},{2,10},{3,11},{4,12},{5,13},{6,14},{7,15},{8,0},{9,1},... | collective-permute-start | bytes 3145736 | tf_op jit(solution)/shard_map/ppermute | solution.py:338
  604.8 35.8 %collective-permute-start.57 = (bf16[2,4,64,1024]{3,2,1,0:T(8,128)(2,1)S(1)}, bf16[2,4,64,1024]{3,2,1,0:T(8,128)(2,1)S(1)}, u32[]{:S(2)}, u32[]{:S(2)}) collective-permute-start(bf16[2,4,64,1024]{3,2,1,0:T(8,128)(2,1)S(1)} %dynamic-slice_bitcast_fusion.1), channel_id=1, source_target_pairs={{0,16},{1,17},{2,18},{3,19},{4,20},{5,21},{6,22},{7,23},{8,24},{9,... | collective-permute-start | bytes 3145736 | tf_op jit(solution)/shard_map/ppermute | solution.py:338
  606.5 34.0 %collective-permute-start.58 = (bf16[1024,256]{1,0:T(8,128)(2,1)}, bf16[1024,256]{1,0:T(8,128)(2,1)S(1)}, u32[]{:S(2)}, u32[]{:S(2)}) collective-permute-start(bf16[1024,256]{1,0:T(8,128)(2,1)} %get-tuple-element.146), channel_id=1, source_target_pairs={{0,4},{1,5},{2,6},{3,7},{4,0},{5,1},{6,2},{7,3},{8,12},{9,13},{10,... | collective-permute-start | bytes 1572872 | tf_op jit(solution)/shard_map/ppermute | solution.py:338
  671.8 57.9 %collective-permute-start.59 = (bf16[1024,768]{1,0:T(8,128)(2,1)}, bf16[1024,768]{1,0:T(8,128)(2,1)}, u32[]{:S(2)}, u32[]{:S(2)}) collective-permute-start(bf16[1024,768]{1,0:T(8,128)(2,1)} %get-tuple-element.204), channel_id=1, source_target_pairs={{0,8},{1,9},{2,10},{3,11},{4,12},{5,13},{6,14},{7,15},{8,0},{9,1},... | collective-permute-start | bytes 4718600 | tf_op jit(solution)/shard_map/ppermute | solution.py:338
  672.6 57.1 %collective-permute-start.61 = (bf16[1024,768]{1,0:T(8,128)(2,1)}, bf16[1024,768]{1,0:T(8,128)(2,1)}, u32[]{:S(2)}, u32[]{:S(2)}) collective-permute-start(bf16[1024,768]{1,0:T(8,128)(2,1)} %get-tuple-element.205), channel_id=1, source_target_pairs={{0,16},{1,17},{2,18},{3,19},{4,20},{5,21},{6,22},{7,23},{8,24},{9,... | collective-permute-start | bytes 4718600 | tf_op jit(solution)/shard_map/ppermute | solution.py:338
  675.2 49.8 %collective-permute-start.64 = (bf16[1,4,64,1024]{3,2,1,0:T(8,128)(2,1)}, bf16[1,4,64,1024]{3,2,1,0:T(8,128)(2,1)}, u32[]{:S(2)}, u32[]{:S(2)}) collective-permute-start(bf16[1,4,64,1024]{3,2,1,0:T(8,128)(2,1)} %constant_dynamic-slice_fusion.1), channel_id=1, source_target_pairs={{0,8},{1,9},{2,10},{3,11},{4,12},{5,13},{6,14},{7,15},{8,0},{9,1},... | collective-permute-start | bytes 1572872 | tf_op jit(solution)/shard_map/ppermute | solution.py:338
  732.4 35.3 %collective-permute-start.62 = (bf16[1024,768]{1,0:T(8,128)(2,1)S(1)}, bf16[1024,768]{1,0:T(8,128)(2,1)S(1)}, u32[]{:S(2)}, u32[]{:S(2)}) collective-permute-start(bf16[1024,768]{1,0:T(8,128)(2,1)S(1)} %get-tuple-element.203), channel_id=1, source_target_pairs={{0,8},{1,9},{2,10},{3,11},{4,12},{5,13},{6,14},{7,15},{8,0},{9,1},... | collective-permute-start | bytes 4718600 | tf_op jit(solution)/shard_map/ppermute | solution.py:338
  733.5 35.1 %collective-permute-start.60 = (bf16[1024,768]{1,0:T(8,128)(2,1)S(1)}, bf16[1024,768]{1,0:T(8,128)(2,1)S(1)}, u32[]{:S(2)}, u32[]{:S(2)}) collective-permute-start(bf16[1024,768]{1,0:T(8,128)(2,1)S(1)} %get-tuple-element.202), channel_id=1, source_target_pairs={{0,16},{1,17},{2,18},{3,19},{4,20},{5,21},{6,22},{7,23},{8,24},{9,... | collective-permute-start | bytes 4718600 | tf_op jit(solution)/shard_map/ppermute | solution.py:338
  (119 other events, 1484.9 us)
Sparse Core Ops, SparseCore 0:
  10.3 102.0 all-gather.2
  653.4 100.9 reduce-scatter.1
